TPU v7x, 256 devices: a whole 4x4x8 slice. The times are simulated.
256 devices in a mesh: row: 16 (over z, x_lo), col: 16 (over y, x_hi, core).
Axes of the slice: x: 4 (x_hi: 2, x_lo: 2; x = x_hi * 2 + x_lo), y: 4, z: 8, core: 2. Of those that a mesh axis runs over, the one named last changes fastest.
Arguments:
- source_points: float32 [32, 32768], P(None, ('row', 'col')), may hold values from -16 to 16, as said below
- target_points: float32 [32, 32768], P(None, 'col'), may hold values from -16 to 16, as said below
- target_potential: float32 [32768], P('col'), may hold values from -3 to 3
Outputs:
- source_new: float32 [32768], P('row')
- target_new: float32 [32768], P('col')
- transport_map: float32 [32, 32768], P(None, ('row', 'col'))
- inverse_map: float32 [32, 32768], P(None, 'col')
Inputs may be any that keep to these rules, and one draw needn't show every extreme that they name: `source_points`: each cell's coordinates are its own independent draws times a scale of that cell, clipped to the range. `target_points`: each cell's coordinates are its own independent draws times a scale of that cell, clipped to the range.
All inputs are finite; a program needn't handle non-finite values.
Results may differ from a plain program's by a relative error of at most 0.0003.
Values sent between devices are 32-bit elements; how exact they have to be, the bound alone decides.
No kernel may reach another device: no remote copies, remote signals or barrier semaphores. Data moves between devices by JAX's collectives and lax.ppermute only.
A program may use at most 64 MiB of HBM per device.

v0:
```python
import math

import jax
import jax.numpy as jnp
from jax import lax
from jax.sharding import PartitionSpec as P

EPS = 0.05


def query_stats(queries, key_points, key_weight, want_mean):
    width = queries.shape[0]
    count = queries.shape[1]
    block_size = math.gcd(count, 512)
    block_count = count // block_size
    query_sq = jnp.sum(queries * queries, axis=0)
    key_sq = jnp.sum(key_points * key_points, axis=0)
    blocked = jnp.transpose(queries.reshape(width, block_count, block_size), (1, 0, 2))
    blocked_sq = query_sq.reshape(block_count, block_size)

    def one_block(pair_in):
        query_block, query_norms = pair_in
        inner_term = jnp.dot(
            query_block.T,
            key_points,
            precision=lax.Precision.HIGHEST,
            preferred_element_type=jnp.float32,
        )
        costs = (query_norms[:, None] + key_sq[None, :] - 2.0 * inner_term) / (2.0 * width)
        scores = (key_weight[None, :] - costs) / EPS
        peaks = jnp.max(scores, axis=1)
        expos = jnp.exp(scores - peaks[:, None])
        totals = jnp.sum(expos, axis=1)
        if want_mean:
            weighted = jnp.dot(
                expos,
                key_points.T,
                precision=lax.Precision.HIGHEST,
                preferred_element_type=jnp.float32,
            )
        else:
            weighted = jnp.zeros((block_size, 1), jnp.float32)
        return (peaks, totals, weighted)

    peaks, totals, weighted = lax.map(one_block, (blocked, blocked_sq))
    peaks = peaks.reshape(count)
    totals = totals.reshape(count)
    weighted = weighted.reshape(count, weighted.shape[2]).T
    return (peaks, totals, weighted)


def local(source_points, target_points, target_potential):
    sources = lax.all_gather(source_points, "col", axis=1, tiled=True)
    source_count = sources.shape[1] * lax.axis_size("row")
    target_count = target_points.shape[1] * lax.axis_size("col")
    peaks, totals, unused = query_stats(sources, target_points, target_potential, False)
    top = lax.pmax(peaks, "col")
    totals = lax.psum(totals * jnp.exp(peaks - top), "col")
    source_new = -EPS * math.log(source_count) - EPS * (top + jnp.log(totals))
    peaks, totals, weighted = query_stats(target_points, sources, source_new, True)
    top = lax.pmax(peaks, "row")
    factor = jnp.exp(peaks - top)
    totals, weighted = lax.psum((totals * factor, weighted * factor[None, :]), "row")
    target_new = -EPS * math.log(target_count) - EPS * (top + jnp.log(totals))
    inverse_map = weighted / totals[None, :]
    peaks, totals, weighted = query_stats(sources, target_points, target_new, True)
    top = lax.pmax(peaks, "col")
    factor = jnp.exp(peaks - top)
    totals, weighted = (
        lax.psum_scatter(totals * factor, "col", scatter_dimension=0, tiled=True),
        lax.psum_scatter(weighted * factor[None, :], "col", scatter_dimension=1, tiled=True),
    )
    transport_map = weighted / totals[None, :]
    return (source_new, target_new, transport_map, inverse_map)


def solution(mesh):
    in_specs = (P(None, ("row", "col")), P(None, "col"), P("col"))
    out_specs = (P("row"), P("col"), P(None, ("row", "col")), P(None, "col"))
    return jax.shard_map(local, mesh=mesh, in_specs=in_specs, out_specs=out_specs, check_vma=False)
```

profile of v0, /device:TPU:1, one launch (start us, length us, event | category | flops | bytes accessed | tf_op | source)
XLA Modules:
  0.0 451.9 jit_solution(8206605945162773017)
XLA Ops:
  8.0 27.0 %all_gather.3 = f32[32,2048]{1,0:T(8,128)S(1)} all-gather(f32[32,128]{1,0:T(8,128)} %param.9), channel_id=1, replica_groups=mesh['row'=16,'col'=16] {'col'}, dimensions={1}, use_global_device_ids=true | all-gather | bytes 278528 | tf_op jit(solution)/shard_map/all_gather | solution.py:53
  35.3 1.0 multiply_reduce_fusion
  36.3 1.1 reshape.70
  37.5 39.3 %while.40 = (s32[]{:T(128)}, f32[4,512]{1,0:T(4,128)S(1)}, f32[4,512]{1,0:T(4,128)S(1)}, f32[2048]{0:T(1024)}, f32[4,512]{1,0:T(4,128)S(1)}, /*index=5*/f32[2048...) while((s32[]{:T(128)}, f32[4,512]{1,0:T(4,128)S(1)}, ...), condition=%wide.region_5.6_spmd, body=%wide.region_2.5_spmd.sunk | while | flops 412089344 | bytes 8753277 | solution.py:45
  37.6 6.8 %fusion.37 = (f32[512]{0:T(512)S(1)}, f32[512,2048]{1,0:T(8,128)}) fusion(f32[32,2048]{1,0:T(8,128)} %get-tuple-element.465, f32[4,32,512]{2,1,0:T(8,128)S(1)} %get-tuple-element.464, s32[]{:T(128)S(6)} %copy.55, f32[2048]{0:T(1024)S(1)} %get-tuple-element.463, f32[512]{0:T(512)S(1)} %bitcast.117, f32[2048]{0:T(1024)} %get-tuple-element.461), kind=kOutput, calls=%fused_computation.38.clone.1 | convolution fusion | flops 409992704 | bytes 4542468 | tf_op jit(solution)/shard_map/while/body/eval_jaxpr/dot_general | solution.py:23
  44.4 2.9 exponential_reduce_fusion.2
  47.4 6.8 %fusion.37 = (f32[512]{0:T(512)S(1)}, f32[512,2048]{1,0:T(8,128)}) fusion(f32[32,2048]{1,0:T(8,128)} %get-tuple-element.465, f32[4,32,512]{2,1,0:T(8,128)S(1)} %get-tuple-element.464, s32[]{:T(128)S(6)} %copy.55, f32[2048]{0:T(1024)S(1)} %get-tuple-element.463, f32[512]{0:T(512)S(1)} %bitcast.117, f32[2048]{0:T(1024)} %get-tuple-element.461), kind=kOutput, calls=%fused_computation.38.clone.1 | convolution fusion | flops 409992704 | bytes 4542468 | tf_op jit(solution)/shard_map/while/body/eval_jaxpr/dot_general | solution.py:23
  54.2 2.9 exponential_reduce_fusion.2
  57.2 6.8 %fusion.37 = (f32[512]{0:T(512)S(1)}, f32[512,2048]{1,0:T(8,128)}) fusion(f32[32,2048]{1,0:T(8,128)} %get-tuple-element.465, f32[4,32,512]{2,1,0:T(8,128)S(1)} %get-tuple-element.464, s32[]{:T(128)S(6)} %copy.55, f32[2048]{0:T(1024)S(1)} %get-tuple-element.463, f32[512]{0:T(512)S(1)} %bitcast.117, f32[2048]{0:T(1024)} %get-tuple-element.461), kind=kOutput, calls=%fused_computation.38.clone.1 | convolution fusion | flops 409992704 | bytes 4542468 | tf_op jit(solution)/shard_map/while/body/eval_jaxpr/dot_general | solution.py:23
  64.1 2.9 exponential_reduce_fusion.2
  67.0 6.8 %fusion.37 = (f32[512]{0:T(512)S(1)}, f32[512,2048]{1,0:T(8,128)}) fusion(f32[32,2048]{1,0:T(8,128)} %get-tuple-element.465, f32[4,32,512]{2,1,0:T(8,128)S(1)} %get-tuple-element.464, s32[]{:T(128)S(6)} %copy.55, f32[2048]{0:T(1024)S(1)} %get-tuple-element.463, f32[512]{0:T(512)S(1)} %bitcast.117, f32[2048]{0:T(1024)} %get-tuple-element.461), kind=kOutput, calls=%fused_computation.38.clone.1 | convolution fusion | flops 409992704 | bytes 4542468 | tf_op jit(solution)/shard_map/while/body/eval_jaxpr/dot_general | solution.py:23
  73.9 2.9 exponential_reduce_fusion.2
  76.9 33.1 %pmax.21 = f32[2048]{0:T(1024)S(1)} all-reduce(f32[2048]{0:T(1024)S(1)} %bitcast.114), channel_id=1, replica_groups=mesh['row'=16,'col'=16] {'col'}, use_global_device_ids=true, to_apply=%region_6.7 | all-reduce | flops 2048 | bytes 16384 | tf_op jit(solution)/shard_map/pmax | solution.py:57
  110.0 34.0 %psum.21 = f32[2048]{0:T(1024)S(1)} all-reduce(f32[2048]{0:T(1024)S(1)} %exponential_multiply_fusion), channel_id=1, replica_groups=mesh['row'=16,'col'=16] {'col'}, use_global_device_ids=true, to_apply=%region_7.8 | all-reduce | flops 2048 | bytes 16384 | tf_op jit(solution)/shard_map/psum | solution.py:58
  144.1 64.9 %while.41 = (s32[]{:T(128)}, f32[4,512]{1,0:T(4,128)S(1)}, f32[4,512]{1,0:T(4,128)S(1)}, f32[4,512,32]{1,0,2:T(4,128)S(1)}, f32[2048]{0:T(1024)S(1)}, /*index=5*...) while((s32[]{:T(128)}, f32[4,512]{1,0:T(4,128)S(1)}, ...), condition=%wide.region_11.12_spmd, body=%wide.region_8.11_spmd.sunk | while | flops 815791104 | bytes 13670537 | solution.py:45
  144.2 5.9 %fusion.40 = (f32[512]{0:T(512)S(1)}, f32[512,2048]{1,0:T(8,128)}) fusion(f32[32,2048]{1,0:T(8,128)S(1)} %get-tuple-element.498, f32[1,32,512]{2,0,1:T(1,128)S(1)} %constant_dynamic-slice_fusion.9, f32[2048]{0:T(1024)S(1)} %get-tuple-element.496, f32[512]{0:T(512)S(1)} %bitcast.116, f32[2048]{0:T(1024)S(1)} %get-tuple-element.494), kind=kOutput, calls=%fused_computation.39.clone.1 | convolution fusion | flops 409992704 | bytes 4542464 | tf_op jit(solution)/shard_map/while/body/eval_jaxpr/dot_general | solution.py:23
  150.2 2.9 fusion.41
  153.1 6.5 %fusion.42 = f32[1,512,32]{1,2,0:T(8,128)S(1)} fusion(f32[32,2048]{1,0:T(8,128)S(1)} %get-tuple-element.498, f32[512,2048]{1,0:T(8,128)} %get-tuple-element.426, f32[512]{0:T(512)S(1)} %get-tuple-element.425), kind=kOutput, calls=%fused_computation.11.clone.1 | convolution fusion | flops 403701760 | bytes 4524032 | tf_op jit(solution)/shard_map/while/body/eval_jaxpr/dot_general | solution.py:35
  160.5 5.9 %fusion.40 = (f32[512]{0:T(512)S(1)}, f32[512,2048]{1,0:T(8,128)}) fusion(f32[32,2048]{1,0:T(8,128)S(1)} %get-tuple-element.498, f32[1,32,512]{2,0,1:T(1,128)S(1)} %constant_dynamic-slice_fusion.9, f32[2048]{0:T(1024)S(1)} %get-tuple-element.496, f32[512]{0:T(512)S(1)} %bitcast.116, f32[2048]{0:T(1024)S(1)} %get-tuple-element.494), kind=kOutput, calls=%fused_computation.39.clone.1 | convolution fusion | flops 409992704 | bytes 4542464 | tf_op jit(solution)/shard_map/while/body/eval_jaxpr/dot_general | solution.py:23
  166.4 2.9 fusion.41
  169.3 6.5 %fusion.42 = f32[1,512,32]{1,2,0:T(8,128)S(1)} fusion(f32[32,2048]{1,0:T(8,128)S(1)} %get-tuple-element.498, f32[512,2048]{1,0:T(8,128)} %get-tuple-element.426, f32[512]{0:T(512)S(1)} %get-tuple-element.425), kind=kOutput, calls=%fused_computation.11.clone.1 | convolution fusion | flops 403701760 | bytes 4524032 | tf_op jit(solution)/shard_map/while/body/eval_jaxpr/dot_general | solution.py:35
  176.7 5.9 %fusion.40 = (f32[512]{0:T(512)S(1)}, f32[512,2048]{1,0:T(8,128)}) fusion(f32[32,2048]{1,0:T(8,128)S(1)} %get-tuple-element.498, f32[1,32,512]{2,0,1:T(1,128)S(1)} %constant_dynamic-slice_fusion.9, f32[2048]{0:T(1024)S(1)} %get-tuple-element.496, f32[512]{0:T(512)S(1)} %bitcast.116, f32[2048]{0:T(1024)S(1)} %get-tuple-element.494), kind=kOutput, calls=%fused_computation.39.clone.1 | convolution fusion | flops 409992704 | bytes 4542464 | tf_op jit(solution)/shard_map/while/body/eval_jaxpr/dot_general | solution.py:23
  182.6 2.9 fusion.41
  185.6 6.5 %fusion.42 = f32[1,512,32]{1,2,0:T(8,128)S(1)} fusion(f32[32,2048]{1,0:T(8,128)S(1)} %get-tuple-element.498, f32[512,2048]{1,0:T(8,128)} %get-tuple-element.426, f32[512]{0:T(512)S(1)} %get-tuple-element.425), kind=kOutput, calls=%fused_computation.11.clone.1 | convolution fusion | flops 403701760 | bytes 4524032 | tf_op jit(solution)/shard_map/while/body/eval_jaxpr/dot_general | solution.py:35
  192.9 5.9 %fusion.40 = (f32[512]{0:T(512)S(1)}, f32[512,2048]{1,0:T(8,128)}) fusion(f32[32,2048]{1,0:T(8,128)S(1)} %get-tuple-element.498, f32[1,32,512]{2,0,1:T(1,128)S(1)} %constant_dynamic-slice_fusion.9, f32[2048]{0:T(1024)S(1)} %get-tuple-element.496, f32[512]{0:T(512)S(1)} %bitcast.116, f32[2048]{0:T(1024)S(1)} %get-tuple-element.494), kind=kOutput, calls=%fused_computation.39.clone.1 | convolution fusion | flops 409992704 | bytes 4542464 | tf_op jit(solution)/shard_map/while/body/eval_jaxpr/dot_general | solution.py:23
  198.9 2.9 fusion.41
  201.8 6.5 %fusion.42 = f32[1,512,32]{1,2,0:T(8,128)S(1)} fusion(f32[32,2048]{1,0:T(8,128)S(1)} %get-tuple-element.498, f32[512,2048]{1,0:T(8,128)} %get-tuple-element.426, f32[512]{0:T(512)S(1)} %get-tuple-element.425), kind=kOutput, calls=%fused_computation.11.clone.1 | convolution fusion | flops 403701760 | bytes 4524032 | tf_op jit(solution)/shard_map/while/body/eval_jaxpr/dot_general | solution.py:35
  209.1 30.0 %pmax.22 = f32[2048]{0:T(1024)S(1)} all-reduce(f32[2048]{0:T(1024)S(1)} %bitcast.110), channel_id=1, replica_groups=mesh['row'=16,'col'=16] {'row'}, use_global_device_ids=true, to_apply=%region_12.13 | all-reduce | flops 2048 | bytes 16384 | tf_op jit(solution)/shard_map/pmax | solution.py:61
  239.3 0.7 multiply_bitcast_fusion
  240.1 25.1 %psum.22 = f32[2048]{0:T(1024)S(1)} all-reduce(f32[2048]{0:T(1024)S(1)} %get-tuple-element.259), channel_id=1, replica_groups=mesh['row'=16,'col'=16] {'row'}, use_global_device_ids=true, to_apply=%region_13.14 | all-reduce | flops 2048 | bytes 16384 | tf_op jit(solution)/shard_map/psum | solution.py:63
  265.3 64.7 %while.42 = (s32[]{:T(128)}, f32[4,512]{1,0:T(4,128)S(1)}, f32[4,512]{1,0:T(4,128)S(1)}, f32[4,512,32]{1,0,2:T(4,128)S(1)}, f32[2048]{0:T(1024)S(1)}, /*index=5*...) while((s32[]{:T(128)}, f32[4,512]{1,0:T(4,128)S(1)}, ...), condition=%wide.region_17.18_spmd, body=%wide.region_14.17_spmd.sunk | while | flops 815791104 | bytes 13539465 | solution.py:45
  265.3 5.9 %fusion.45 = (f32[512]{0:T(512)S(1)}, f32[512,2048]{1,0:T(8,128)}) fusion(f32[32,2048]{1,0:T(8,128)S(1)} %get-tuple-element.531, f32[4,32,512]{2,1,0:T(8,128)S(1)} %get-tuple-element.530, s32[]{:T(128)S(6)} %copy.77, f32[2048]{0:T(1024)S(1)} %get-tuple-element.529, f32[512]{0:T(512)S(1)} %bitcast.118, f32[2048]{0:T(1024)S(1)} %get-tuple-element.527), kind=kOutput, calls=%fused_computation.40.clone.1 | convolution fusion | flops 409992704 | bytes 4542468 | tf_op jit(solution)/shard_map/while/body/eval_jaxpr/dot_general | solution.py:23
  271.2 2.9 fusion.46
  274.2 6.6 %fusion.47 = f32[1,512,32]{1,2,0:T(8,128)S(1)} fusion(f32[32,2048]{1,0:T(8,128)S(1)} %get-tuple-element.531, f32[512,2048]{1,0:T(8,128)} %get-tuple-element.437, f32[512]{0:T(512)S(1)} %get-tuple-element.436), kind=kOutput, calls=%fused_computation.20.clone.1 | convolution fusion | flops 403701760 | bytes 4524032 | tf_op jit(solution)/shard_map/while/body/eval_jaxpr/dot_general | solution.py:35
  281.5 5.9 %fusion.45 = (f32[512]{0:T(512)S(1)}, f32[512,2048]{1,0:T(8,128)}) fusion(f32[32,2048]{1,0:T(8,128)S(1)} %get-tuple-element.531, f32[4,32,512]{2,1,0:T(8,128)S(1)} %get-tuple-element.530, s32[]{:T(128)S(6)} %copy.77, f32[2048]{0:T(1024)S(1)} %get-tuple-element.529, f32[512]{0:T(512)S(1)} %bitcast.118, f32[2048]{0:T(1024)S(1)} %get-tuple-element.527), kind=kOutput, calls=%fused_computation.40.clone.1 | convolution fusion | flops 409992704 | bytes 4542468 | tf_op jit(solution)/shard_map/while/body/eval_jaxpr/dot_general | solution.py:23
  287.4 2.9 fusion.46
  290.4 6.6 %fusion.47 = f32[1,512,32]{1,2,0:T(8,128)S(1)} fusion(f32[32,2048]{1,0:T(8,128)S(1)} %get-tuple-element.531, f32[512,2048]{1,0:T(8,128)} %get-tuple-element.437, f32[512]{0:T(512)S(1)} %get-tuple-element.436), kind=kOutput, calls=%fused_computation.20.clone.1 | convolution fusion | flops 403701760 | bytes 4524032 | tf_op jit(solution)/shard_map/while/body/eval_jaxpr/dot_general | solution.py:35
  297.7 5.9 %fusion.45 = (f32[512]{0:T(512)S(1)}, f32[512,2048]{1,0:T(8,128)}) fusion(f32[32,2048]{1,0:T(8,128)S(1)} %get-tuple-element.531, f32[4,32,512]{2,1,0:T(8,128)S(1)} %get-tuple-element.530, s32[]{:T(128)S(6)} %copy.77, f32[2048]{0:T(1024)S(1)} %get-tuple-element.529, f32[512]{0:T(512)S(1)} %bitcast.118, f32[2048]{0:T(1024)S(1)} %get-tuple-element.527), kind=kOutput, calls=%fused_computation.40.clone.1 | convolution fusion | flops 409992704 | bytes 4542468 | tf_op jit(solution)/shard_map/while/body/eval_jaxpr/dot_general | solution.py:23
  303.6 2.9 fusion.46
  306.5 6.5 %fusion.47 = f32[1,512,32]{1,2,0:T(8,128)S(1)} fusion(f32[32,2048]{1,0:T(8,128)S(1)} %get-tuple-element.531, f32[512,2048]{1,0:T(8,128)} %get-tuple-element.437, f32[512]{0:T(512)S(1)} %get-tuple-element.436), kind=kOutput, calls=%fused_computation.20.clone.1 | convolution fusion | flops 403701760 | bytes 4524032 | tf_op jit(solution)/shard_map/while/body/eval_jaxpr/dot_general | solution.py:35
  313.9 5.9 %fusion.45 = (f32[512]{0:T(512)S(1)}, f32[512,2048]{1,0:T(8,128)}) fusion(f32[32,2048]{1,0:T(8,128)S(1)} %get-tuple-element.531, f32[4,32,512]{2,1,0:T(8,128)S(1)} %get-tuple-element.530, s32[]{:T(128)S(6)} %copy.77, f32[2048]{0:T(1024)S(1)} %get-tuple-element.529, f32[512]{0:T(512)S(1)} %bitcast.118, f32[2048]{0:T(1024)S(1)} %get-tuple-element.527), kind=kOutput, calls=%fused_computation.40.clone.1 | convolution fusion | flops 409992704 | bytes 4542468 | tf_op jit(solution)/shard_map/while/body/eval_jaxpr/dot_general | solution.py:23
  319.8 2.9 fusion.46
  322.7 6.5 %fusion.47 = f32[1,512,32]{1,2,0:T(8,128)S(1)} fusion(f32[32,2048]{1,0:T(8,128)S(1)} %get-tuple-element.531, f32[512,2048]{1,0:T(8,128)} %get-tuple-element.437, f32[512]{0:T(512)S(1)} %get-tuple-element.436), kind=kOutput, calls=%fused_computation.20.clone.1 | convolution fusion | flops 403701760 | bytes 4524032 | tf_op jit(solution)/shard_map/while/body/eval_jaxpr/dot_general | solution.py:35
  330.2 47.2 %pmax.23 = f32[2048]{0:T(1024)S(1)} all-reduce(f32[2048]{0:T(1024)S(1)} %bitcast.112), channel_id=1, replica_groups=mesh['row'=16,'col'=16] {'col'}, use_global_device_ids=true, to_apply=%region_18.19 | all-reduce | flops 2048 | bytes 16384 | tf_op jit(solution)/shard_map/pmax | solution.py:67
  378.1 33.8 %all-reduce = f32[2048]{0:T(1024)S(1)} all-reduce(f32[2048]{0:T(1024)S(1)} %get-tuple-element.257), channel_id=3, replica_groups=mesh['row'=16,'col'=16] {'col'}, use_global_device_ids=true, to_apply=%region_20.21.clone | all-reduce | flops 2048 | bytes 16384
  413.3 1.7 broadcast_divide_fusion
  415.0 28.1 %reduce-scatter.2.cloned.1.call-done = f32[32,128]{1,0:T(8,128)} async-done(((f32[32,2048]{1,0:T(8,128)}), f32[32,128]{1,0:T(8,128)}) %reduce-scatter.2.cloned.1.call-update) | async-done | bytes 16400 | tf_op jit(solution)/shard_map/reduce_scatter | solution.py:71
  443.1 1.3 broadcast_divide_fusion.1
  (98 shorter events, 9.2 us)
Async XLA Ops:
  8.0 405.3 %all-reduce.3.cloned.1.call-start = ((), (), s32[]{:S(2)}) async-start(), calls=%async_computation.2 | async-start | bytes 524288 | tf_op jit(solution)/shard_map/psum | solution.py:63
  144.1 121.1 %copy-start = (f32[32,2048]{1,0:T(8,128)S(1)}, f32[32,2048]{1,0:T(8,128)}, u32[]{:S(2)}) copy-start(f32[32,2048]{1,0:T(8,128)} %get-tuple-element.536) | copy-start | bytes 786436
  209.1 56.2 %copy-start.1 = (f32[2048]{0:T(1024)}, f32[2048]{0:T(1024)S(1)}, u32[]{:S(2)}) copy-start(f32[2048]{0:T(1024)S(1)} %get-tuple-element.546) | copy-start | bytes 24580
  240.0 203.1 %reduce-scatter.2.cloned.1.call-start = ((), (), s32[]{:S(2)}) async-start(), calls=%async_computation.1 | async-start | bytes 278528 | tf_op jit(solution)/shard_map/reduce_scatter | solution.py:71
  265.3 146.7 %copy-start.3 = (u32[256]{0:T(256)S(1)}, u32[256]{0:T(256)}, u32[]{:S(2)}) copy-start(u32[256]{0:T(256)} %constant.82) | copy-start | bytes 3076
  330.0 114.4 %copy-start.2 = (f32[2048]{0:T(1024)}, f32[2048]{0:T(1024)S(1)}, u32[]{:S(2)}) copy-start(f32[2048]{0:T(1024)S(1)} %get-tuple-element.547) | copy-start | bytes 24580
Sparse Core Ops, SparseCore 0:
  240.2 126.5 all-reduce.2
Sparse Core Ops, SparseCore 1:
  378.2 64.9 reduce-scatter.1
where the time goes:
time: 454 us; the launch traced here: 452 us
  blocking collectives  230 us (51%)
  matrix products  127 us (28%)
  other arithmetic  40.2 us (9%)
  waiting for transfers between devices  28.2 us (6%)
  between operations  16.5 us (4%)
  local copies, waits for them, and re-layouts  9.45 us (2%)
    pmax x2, blocking collectives, local(): top = lax.pmax(peaks, 'col')  80.4 us
    dot_general x12, matrix products, one_block(): jnp.dot(query_block.T, key_points, precision=lax.Precision.HIGHEST, prefe...  74.3 us
    dot_general x8, matrix products, one_block(): jnp.dot(expos, key_points.T, precision=lax.Precision.HIGHEST, preferred_e...  52.4 us
    reduce_sum x12, other arithmetic, one_block(): totals = jnp.sum(expos, axis=1)  34.7 us
    psum x1, blocking collectives, local(): totals = lax.psum(totals * jnp.exp(peaks - top), 'col')  34 us
    unnamed x1, blocking collectives  33.8 us
    pmax x1, blocking collectives, local(): top = lax.pmax(peaks, 'row')  30 us
    reduce_scatter x1, waiting for transfers between devices, local(): lax.psum_scatter(weighted * factor[None, :], 'col', scatter_dimension=1,...  28.1 us
  transfers between devices with their start and end apart: 2, of which 1 were waited for; matrix products, arithmetic and copies ran while one was open for 15% of the time, Pallas kernels for 0%

commit v1 on v0

v1 whole, which is shorter than its diff:
```python
import functools
import math

import jax
import jax.numpy as jnp
from jax import lax
from jax.experimental import pallas as pl
from jax.experimental.pallas import tpu as pltpu
from jax.sharding import PartitionSpec as P

EPS = 0.05
F32 = jnp.float32
BF16 = jnp.bfloat16
LANES = 128
TILE = 256
LOG2E = math.log2(math.e)
VMEM_LIMIT = 48 * 1024 * 1024


def split(value, parts):
    out = []
    for _ in range(parts):
        part = value.astype(BF16)
        out.append(part)
        value = value - part.astype(F32)
    return out


def weight_rows(first, second):
    width = (first if first is not None else second).shape[1]
    row = lax.broadcasted_iota(jnp.int32, (16, width), 0)
    out = jnp.zeros((16, width), F32)
    for at, value in ((0, first), (3, second)):
        if value is None:
            out = jnp.where((row >= at) & (row < at + 3), 1.0, out)
        else:
            for k, part in enumerate(split(value, 3)):
                out = jnp.where(row == at + k, part.astype(F32), out)
    return out.astype(BF16)


def key_stack(points, weight):
    a, b, c = split(points, 3)
    return jnp.concatenate([a, b, a, c, a, b, weight_rows(weight, None)], axis=0)


def query_stack(points, weight):
    a, b, c = split(points, 3)
    zero = jnp.zeros((1, points.shape[1]), F32) if weight is None else weight
    return jnp.concatenate([a, a, b, a, c, b, weight_rows(None, zero)], axis=0)


def mean_rows(points):
    a, b, c = split(points, 3)
    ones = weight_rows(None, jnp.zeros((1, points.shape[1]), F32))
    keep = lax.broadcasted_iota(jnp.int32, ones.shape, 0) == 0
    ones = jnp.where(keep, ones.astype(F32), 0.0).astype(BF16)
    return jnp.concatenate([a, ones, b, c], axis=0)


def dot(a, b):
    return jnp.dot(a, b, preferred_element_type=F32)


def chunk_row(ref, chunks):
    return jnp.concatenate([ref[c] for c in range(chunks)], axis=1)


def peak8(scores):
    rows, cols = scores.shape
    return jnp.max(scores.reshape(rows // 8, 8, cols), axis=0)


def scores_tile(keys, queries, scores, slot, at):
    q = queries[:, pl.ds(pl.multiple_of(at * TILE, TILE), TILE)]
    peak = None
    for k in range(keys.shape[0] // TILE):
        s = dot(keys[k * TILE : (k + 1) * TILE, :], q)
        scores[slot, k * TILE : (k + 1) * TILE, :] = s
        p = peak8(s)
        peak = p if peak is None else jnp.maximum(peak, p)
    return jnp.max(peak, axis=0, keepdims=True)


def weighted(expos, means, k, sums):
    high = expos.astype(BF16)
    low = (expos - high.astype(F32)).astype(BF16)
    m = means[:, k * TILE : (k + 1) * TILE]
    full = dot(m, high)
    rest = dot(m[:80], low)
    part = full[:48] + rest[:48]
    tail = full[48:80] + full[80:112] + rest[48:80]
    return (part, tail) if sums is None else (sums[0] + part, sums[1] + tail)


def pipelined(steps, first, second):
    peak = first(0, 0)

    def step(at, peak):
        later = first(at, at % 2)
        second(at - 1, (at - 1) % 2, peak)
        return later

    peak = lax.fori_loop(1, steps, step, peak)
    second(steps - 1, (steps - 1) % 2, peak)


def forward_kernel(scale, x_ref, y_ref, g_ref, out_ref, keys, queries, scores):
    count = y_ref.shape[1]
    y = y_ref[...]
    weight = g_ref[...] * (LOG2E / EPS) - scale * jnp.sum(y * y, axis=0, keepdims=True)
    keys[...] = key_stack(y, weight).T
    chunks = x_ref.shape[0]
    queries[...] = query_stack(chunk_row(x_ref, chunks) * (2.0 * scale), None)

    def first(at, slot):
        return scores_tile(keys, queries, scores, slot, at)

    def second(at, slot, peak):
        total = None
        for k in range(count // TILE):
            e = jnp.exp2(scores[slot, k * TILE : (k + 1) * TILE, :] - peak)
            t = jnp.sum(e.reshape(TILE // 8, 8, TILE), axis=0)
            total = t if total is None else total + t
        total = jnp.sum(total, axis=0, keepdims=True)
        pair = jnp.concatenate([peak, total], axis=0)
        lanes = pl.ds(pl.multiple_of(at * TILE, TILE), TILE)
        for c in range(out_ref.shape[0]):
            out_ref[c, :, lanes] = pair

    pipelined(queries.shape[1] // TILE, first, second)


def backward_kernel(scale, total_count, x_ref, y_ref, stats_ref, out_ref, f_ref, h_ref, keys, queries, scores, means, lse):
    chunks = x_ref.shape[0]
    x = chunk_row(x_ref, chunks)
    peaks = stats_ref[:, 0, :]
    top = jnp.max(peaks, axis=0, keepdims=True)
    total = jnp.sum(stats_ref[:, 1, :] * jnp.exp2(peaks - top), axis=0, keepdims=True)
    h = -math.log2(total_count) - (top + jnp.log2(total))
    h_ref[...] = h
    f_ref[...] = (EPS / LOG2E) * (h + scale * jnp.sum(x * x, axis=0, keepdims=True))
    keys[...] = key_stack(x, h).T
    queries[...] = query_stack(y_ref[...] * (2.0 * scale), None)
    means[...] = mean_rows(x)

    def first(at, slot):
        return scores_tile(keys, queries, scores, slot, at)

    def second(at, slot, peak):
        sums = None
        for k in range(keys.shape[0] // TILE):
            e = jnp.exp2(scores[slot, k * TILE : (k + 1) * TILE, :] - peak)
            sums = weighted(e, means, k, sums)
        total = sums[0][32:33]
        mean = (sums[0][:32] + sums[1]) / total
        value = peak + jnp.log2(total)
        for c in range(TILE // LANES):
            cut = slice(c * LANES, (c + 1) * LANES)
            out_ref[at * (TILE // LANES) + c, :32, :] = mean[:, cut]
            lse[pl.ds(at * (TILE // LANES) + c, 1), :] = value[:, cut]

    pipelined(queries.shape[1] // TILE, first, second)
    rows = lse[...]
    for c in range(out_ref.shape[0]):
        out_ref[c, 32:, :] = rows


def reduce_kernel(in_ref, out_ref, lse_ref):
    me = lax.axis_index("row")
    every = in_ref[:, 32:, :]
    top = jnp.max(every, axis=0)
    lse_ref[...] = top + jnp.log2(jnp.sum(jnp.exp2(every - top[None]), axis=0))
    mine = in_ref[:, pl.ds(32 + me, 1), :]
    share = jnp.exp2(mine - lse_ref[pl.ds(me, 1), :][None])
    value = jnp.sum(in_ref[:, :32, :] * share, axis=0)
    for c in range(out_ref.shape[0]):
        out_ref[c] = value


def plan_kernel(scale, total_count, x_ref, y_ref, h_ref, lse_ref, out_ref, g_ref, keys, queries, means):
    y = y_ref[...]
    lse = jnp.concatenate([lse_ref[c : c + 1, :] for c in range(lse_ref.shape[0])], axis=1)
    y_sq = jnp.sum(y * y, axis=0, keepdims=True)
    g_ref[...] = (EPS / LOG2E) * (scale * y_sq - math.log2(total_count) - lse)
    keys[...] = key_stack(y, -lse).T
    chunks = x_ref.shape[0]
    queries[...] = query_stack(chunk_row(x_ref, chunks) * (2.0 * scale), h_ref[...])
    means[...] = mean_rows(y)

    def step(at, carry):
        q = queries[:, pl.ds(pl.multiple_of(at * TILE, TILE), TILE)]
        sums = None
        for k in range(keys.shape[0] // TILE):
            e = jnp.exp2(dot(keys[k * TILE : (k + 1) * TILE, :], q))
            sums = weighted(e, means, k, sums)
        for c in range(TILE // LANES):
            cut = slice(c * LANES, (c + 1) * LANES)
            out_ref[at * (TILE // LANES) + c, :32, :] = sums[0][:32, cut] + sums[1][:, cut]
            out_ref[at * (TILE // LANES) + c, 32:, :] = sums[0][32:40, cut]
        return carry

    lax.fori_loop(0, queries.shape[1] // TILE, step, 0)


def finish_kernel(in_ref, inv_ref, out_ref, inv_out_ref):
    sums = jnp.sum(in_ref[...], axis=0)
    out_ref[...] = sums[:32] / sums[32:33]
    for c in range(inv_ref.shape[0]):
        inv_out_ref[:, c * LANES : (c + 1) * LANES] = inv_ref[c]


def call(body, outs, scratch, flops, *args):
    return pl.pallas_call(
        body,
        out_shape=[jax.ShapeDtypeStruct(s, F32) for s in outs],
        in_specs=[pl.BlockSpec(memory_space=pltpu.VMEM)] * len(args),
        out_specs=[pl.BlockSpec(memory_space=pltpu.VMEM)] * len(outs),
        scratch_shapes=scratch,
        compiler_params=pltpu.CompilerParams(vmem_limit_bytes=VMEM_LIMIT),
        cost_estimate=pl.CostEstimate(flops=flops, bytes_accessed=1 << 20, transcendentals=0),
    )(*args)


def local(source_points, target_points, target_potential):
    width, own = source_points.shape
    cols, rows = lax.axis_size("col"), lax.axis_size("row")
    n, m = own * cols, target_points.shape[1]
    source_count, target_count = n * rows, m * cols
    scale = LOG2E / (2.0 * width * EPS)
    depth = 6 * width + 16
    keys = pltpu.VMEM((m, depth), BF16)
    queries = pltpu.VMEM((depth, n), BF16)
    scores = pltpu.VMEM((2, m, TILE), F32)
    means = pltpu.VMEM((3 * width + 16, m), BF16)
    flops = 2 * n * m * 256

    x = lax.all_to_all(jnp.broadcast_to(source_points, (cols, width, own)), "col", 0, 0)
    (stats,) = call(
        functools.partial(forward_kernel, scale),
        [(cols, 2, n)],
        [keys, queries, scores],
        flops,
        x,
        target_points,
        target_potential.reshape(1, m),
    )
    stats = lax.all_to_all(stats, "col", 0, 0)
    partial, f, h = call(
        functools.partial(backward_kernel, scale, target_count),
        [(rows, width + rows, m // rows), (1, n), (1, n)],
        [keys, queries, scores, means, pltpu.VMEM((rows, m // rows), F32)],
        2 * flops,
        x,
        target_points,
        stats,
    )
    partial = lax.all_to_all(partial, "row", 0, 0)
    inverse, lse = call(reduce_kernel, [(rows, width, m // rows), (rows, m // rows)], [], 1 << 20, partial)
    inverse = lax.all_to_all(inverse, "row", 0, 0)
    plan, g = call(
        functools.partial(plan_kernel, scale, source_count),
        [(cols, width + 8, own), (1, m)],
        [keys, queries, means],
        2 * flops,
        x,
        target_points,
        h,
        lse,
    )
    plan = lax.all_to_all(plan, "col", 0, 0)
    transport_map, inverse_map = call(finish_kernel, [(width, own), (width, m)], [], 1 << 20, plan, inverse)
    return f.reshape(n), g.reshape(m), transport_map, inverse_map


def solution(mesh):
    in_specs = (P(None, ("row", "col")), P(None, "col"), P("col"))
    out_specs = (P("row"), P("col"), P(None, ("row", "col")), P(None, "col"))
    return jax.shard_map(local, mesh=mesh, in_specs=in_specs, out_specs=out_specs, check_vma=False)
```

time: 454 us -> 113 us (0.25)
  blocking collectives: 230 us -> 78.6 us
  matrix products: 127 us -> 0 us
  other arithmetic: 40.2 us -> 0 us
  Pallas kernels: 0 us -> 31.5 us
  waiting for transfers between devices: 28.2 us -> 0 us
  between operations: 16.5 us -> 0.68 us
  local copies, waits for them, and re-layouts: 9.45 us -> 0.75 us
    dot_general x20 -> x0, matrix products: 127 us -> none  [the longest x12 74.3 us: one_block(): jnp.dot(query_block.T, key_points, precision=lax.Precision.HIGHEST, prefe...]
    pmax x3 -> x0, blocking collectives: 110 us -> none  [the longest x2 80.4 us: local(): top = lax.pmax(peaks, 'col')]
    all_to_all x0 -> x5, blocking collectives: none -> 78.6 us  [the longest x1 21 us: local(): partial = lax.all_to_all(partial, 'row', 0, 0)]
    psum x2 -> x0, blocking collectives: 59.1 us -> none  [the longest x1 34 us: local(): totals = lax.psum(totals * jnp.exp(peaks - top), 'col')]
    reduce_sum x14 -> x0, other arithmetic: 35.7 us -> none  [the longest x12 34.7 us: one_block(): totals = jnp.sum(expos, axis=1)]
    unnamed x1 -> x0, blocking collectives: 33.8 us -> none
    pallas_call x0 -> x5, Pallas kernels: none -> 31.5 us  [call(): pl.pallas_call(body, out_shape=[jax.ShapeDtypeStruct(s, F32) for s in out...]
    reduce_scatter x1 -> x0, waiting for transfers between devices: 28.1 us -> none  [local(): lax.psum_scatter(weighted * factor[None, :], 'col', scatter_dimension=1,...]
  transfers between devices with their start and end apart: 2 -> 0, of which waited for: 1 -> 0; matrix products, arithmetic and copies ran while one was open for 15% -> 0% of each run, Pallas kernels for 0% -> 0%
where the time goes in v1:
time: 113 us; the launch traced here: 112 us
  blocking collectives  78.6 us (70%)
  Pallas kernels  31.5 us (28%)
    pallas_call x5, Pallas kernels, call(): pl.pallas_call(body, out_shape=[jax.ShapeDtypeStruct(s, F32) for s in out...  31.5 us
    all_to_all x1, blocking collectives, local(): partial = lax.all_to_all(partial, 'row', 0, 0)  21 us
    all_to_all x1, blocking collectives, local(): lax.all_to_all(jnp.broadcast_to(source_points, (cols, width, own)), 'col'...  17 us
    all_to_all x1, blocking collectives, local(): plan = lax.all_to_all(plan, 'col', 0, 0)  15.8 us
    all_to_all x1, blocking collectives, local(): inverse = lax.all_to_all(inverse, 'row', 0, 0)  12.7 us
    all_to_all x1, blocking collectives, local(): stats = lax.all_to_all(stats, 'col', 0, 0)  12.1 us

profile of v1, /device:TPU:1, one launch (start us, length us, event | category | flops | bytes accessed | tf_op | source)
XLA Modules:
  0.0 111.6 jit_solution(8562853566409133922)
XLA Ops:
  0.6 0.7 broadcast_in_dim.3
  1.4 0.0 copy-start
  1.4 0.0 copy-start.1
  1.4 17.0 %all_to_all.25.x_ref = f32[16,32,128]{2,1,0:T(8,128)S(1)} all-to-all(f32[16,32,128]{2,1,0:T(8,128)S(1)} %broadcast_in_dim.3), channel_id=1, replica_groups=mesh['row'=16,'col'=16] {'col'}, dimensions={0} | all-to-all | bytes 524288 | tf_op jit(solution)/shard_map/all_to_all | solution.py:238
  18.4 0.0 copy-done
  18.4 0.0 copy-done.1
  18.4 7.6 %shard_map.66 = f32[16,2,2048]{2,1,0:T(2,128)S(1)} custom-call(f32[16,32,128]{2,1,0:T(8,128)S(1)} %all_to_all.25.x_ref, f32[32,2048]{1,0:T(8,128)S(1)} %copy-done, f32[1,2048]{1,0:T(1,128)S(1)} %bitcast.3), custom_call_target="tpu_custom_call" | custom-call | flops 2147483648 | bytes 1048576 | tf_op jit(solution)/shard_map/pallas_call | solution.py:214
  26.1 12.1 %all_to_all.26.stats_ref = f32[16,2,2048]{2,1,0:T(2,128)S(1)} all-to-all(f32[16,2,2048]{2,1,0:T(2,128)S(1)} %shard_map.66), channel_id=1, replica_groups=mesh['row'=16,'col'=16] {'col'}, dimensions={0} | all-to-all | bytes 524288 | tf_op jit(solution)/shard_map/all_to_all | solution.py:248
  38.2 15.7 %shard_map.67 = (f32[16,48,128]{2,1,0:T(8,128)S(1)}, f32[1,2048]{1,0:T(1,128)}, f32[1,2048]{1,0:T(1,128)S(1)}) custom-call(f32[16,32,128]{2,1,0:T(8,128)S(1)} %all_to_all.25.x_ref, f32[32,2048]{1,0:T(8,128)S(1)} %copy-done, f32[16,2,2048]{2,1,0:T(2,128)S(1)} %all_to_all.26.stats_ref), custom_call_target="tpu_custom_call" | custom-call | flops 4294967296 | bytes 1048576 | tf_op jit(solution)/shard_map/pallas_call | solution.py:214
  53.9 21.0 %all_to_all.27.in_ref = f32[16,48,128]{2,1,0:T(8,128)S(1)} all-to-all(f32[16,48,128]{2,1,0:T(8,128)S(1)} %get-tuple-element.15), channel_id=1, replica_groups=mesh['row'=16,'col'=16] {'row'}, dimensions={0} | all-to-all | bytes 786432 | tf_op jit(solution)/shard_map/all_to_all | solution.py:258
  74.8 0.1 shard_map.68
  74.9 7.4 %shard_map.69 = (f32[16,40,128]{2,1,0:T(8,128)S(1)}, f32[1,2048]{1,0:T(1,128)}) custom-call(f32[16,32,128]{2,1,0:T(8,128)S(1)} %all_to_all.25.x_ref, f32[32,2048]{1,0:T(8,128)S(1)} %copy-done, f32[1,2048]{1,0:T(1,128)S(1)} %get-tuple-element.14.h_ref, f32[16,128]{1,0:T(8,128)S(1)} %get-tuple-element.16.lse_ref), custom_call_target="tpu_custom_call" | custom-call | flops 4294967296 | bytes 1048576 | tf_op jit(solution)/shard_map/pallas_call | solution.py:214
  82.4 15.8 %all_to_all.28.in_ref = f32[16,40,128]{2,1,0:T(8,128)S(1)} all-to-all(f32[16,40,128]{2,1,0:T(8,128)S(1)} %get-tuple-element.18), channel_id=1, replica_groups=mesh['row'=16,'col'=16] {'col'}, dimensions={0} | all-to-all | bytes 655360 | tf_op jit(solution)/shard_map/all_to_all | solution.py:271
  98.2 12.7 %all_to_all.29.inv_ref = f32[16,32,128]{2,1,0:T(8,128)S(1)} all-to-all(f32[16,32,128]{2,1,0:T(8,128)S(1)} %get-tuple-element.19), channel_id=1, replica_groups=mesh['row'=16,'col'=16] {'row'}, dimensions={0} | all-to-all | bytes 524288 | tf_op jit(solution)/shard_map/all_to_all | solution.py:260
  110.8 0.7 shard_map.70
Async XLA Ops:
  1.4 17.1 %copy-start = (f32[32,2048]{1,0:T(8,128)S(1)}, f32[32,2048]{1,0:T(8,128)}, u32[]{:S(2)}) copy-start(f32[32,2048]{1,0:T(8,128)} %y_ref.5) | copy-start | bytes 786436
  1.4 17.1 %copy-start.1 = (f32[2048]{0:T(1024)S(1)}, f32[2048]{0:T(1024)}, u32[]{:S(2)}) copy-start(f32[2048]{0:T(1024)} %param.5) | copy-start | bytes 24580

commit v2 on v1

--- a/solution.py
+++ b/solution.py
@@ -13,6 +13,7 @@
 BF16 = jnp.bfloat16
 LANES = 128
 TILE = 256
+BLOCK = 512
 LOG2E = math.log2(math.e)
 VMEM_LIMIT = 48 * 1024 * 1024
 
@@ -71,12 +72,12 @@
     return jnp.max(scores.reshape(rows // 8, 8, cols), axis=0)
 
 
-def scores_tile(keys, queries, scores, slot, at):
-    q = queries[:, pl.ds(pl.multiple_of(at * TILE, TILE), TILE)]
+def scores_tile(keys, queries, scores, at):
+    q = queries[:, at * TILE : (at + 1) * TILE]
     peak = None
-    for k in range(keys.shape[0] // TILE):
-        s = dot(keys[k * TILE : (k + 1) * TILE, :], q)
-        scores[slot, k * TILE : (k + 1) * TILE, :] = s
+    for k in range(keys.shape[0] // BLOCK):
+        s = dot(keys[k * BLOCK : (k + 1) * BLOCK, :], q)
+        scores[at % 2, k * BLOCK : (k + 1) * BLOCK, :] = s
         p = peak8(s)
         peak = p if peak is None else jnp.maximum(peak, p)
     return jnp.max(peak, axis=0, keepdims=True)
@@ -85,7 +86,7 @@
 def weighted(expos, means, k, sums):
     high = expos.astype(BF16)
     low = (expos - high.astype(F32)).astype(BF16)
-    m = means[:, k * TILE : (k + 1) * TILE]
+    m = means[:, k * BLOCK : (k + 1) * BLOCK]
     full = dot(m, high)
     rest = dot(m[:80], low)
     part = full[:48] + rest[:48]
@@ -94,15 +95,11 @@
 
 
 def pipelined(steps, first, second):
-    peak = first(0, 0)
-
-    def step(at, peak):
-        later = first(at, at % 2)
-        second(at - 1, (at - 1) % 2, peak)
-        return later
-
-    peak = lax.fori_loop(1, steps, step, peak)
-    second(steps - 1, (steps - 1) % 2, peak)
+    peak = first(0)
+    for at in range(steps):
+        later = first(at + 1) if at + 1 < steps else None
+        second(at, peak)
+        peak = later
 
 
 def forward_kernel(scale, x_ref, y_ref, g_ref, out_ref, keys, queries, scores):
@@ -113,25 +110,24 @@
     chunks = x_ref.shape[0]
     queries[...] = query_stack(chunk_row(x_ref, chunks) * (2.0 * scale), None)
 
-    def first(at, slot):
-        return scores_tile(keys, queries, scores, slot, at)
-
-    def second(at, slot, peak):
+    def first(at):
+        return scores_tile(keys, queries, scores, at)
+
+    def second(at, peak):
         total = None
-        for k in range(count // TILE):
-            e = jnp.exp2(scores[slot, k * TILE : (k + 1) * TILE, :] - peak)
-            t = jnp.sum(e.reshape(TILE // 8, 8, TILE), axis=0)
+        for k in range(count // BLOCK):
+            e = jnp.exp2(scores[at % 2, k * BLOCK : (k + 1) * BLOCK, :] - peak)
+            t = jnp.sum(e.reshape(BLOCK // 8, 8, TILE), axis=0)
             total = t if total is None else total + t
         total = jnp.sum(total, axis=0, keepdims=True)
         pair = jnp.concatenate([peak, total], axis=0)
-        lanes = pl.ds(pl.multiple_of(at * TILE, TILE), TILE)
         for c in range(out_ref.shape[0]):
-            out_ref[c, :, lanes] = pair
+            out_ref[c, :, at * TILE : (at + 1) * TILE] = pair
 
     pipelined(queries.shape[1] // TILE, first, second)
 
 
-def backward_kernel(scale, total_count, x_ref, y_ref, stats_ref, out_ref, f_ref, h_ref, keys, queries, scores, means, lse):
+def backward_kernel(scale, total_count, x_ref, y_ref, stats_ref, out_ref, f_ref, h_ref, keys, queries, scores, means):
     chunks = x_ref.shape[0]
     x = chunk_row(x_ref, chunks)
     peaks = stats_ref[:, 0, :]
@@ -144,70 +140,63 @@
     queries[...] = query_stack(y_ref[...] * (2.0 * scale), None)
     means[...] = mean_rows(x)
 
-    def first(at, slot):
-        return scores_tile(keys, queries, scores, slot, at)
-
-    def second(at, slot, peak):
+    def first(at):
+        return scores_tile(keys, queries, scores, at)
+
+    def second(at, peak):
         sums = None
-        for k in range(keys.shape[0] // TILE):
-            e = jnp.exp2(scores[slot, k * TILE : (k + 1) * TILE, :] - peak)
+        for k in range(keys.shape[0] // BLOCK):
+            e = jnp.exp2(scores[at % 2, k * BLOCK : (k + 1) * BLOCK, :] - peak)
             sums = weighted(e, means, k, sums)
         total = sums[0][32:33]
         mean = (sums[0][:32] + sums[1]) / total
-        value = peak + jnp.log2(total)
+        value = jnp.broadcast_to(peak + jnp.log2(total), (8, TILE))
         for c in range(TILE // LANES):
             cut = slice(c * LANES, (c + 1) * LANES)
             out_ref[at * (TILE // LANES) + c, :32, :] = mean[:, cut]
-            lse[pl.ds(at * (TILE // LANES) + c, 1), :] = value[:, cut]
+            out_ref[at * (TILE // LANES) + c, 32:, :] = value[:, cut]
 
     pipelined(queries.shape[1] // TILE, first, second)
-    rows = lse[...]
-    for c in range(out_ref.shape[0]):
-        out_ref[c, 32:, :] = rows
-
-
-def reduce_kernel(in_ref, out_ref, lse_ref):
-    me = lax.axis_index("row")
+
+
+def reduce_kernel(in_ref, out_ref):
     every = in_ref[:, 32:, :]
     top = jnp.max(every, axis=0)
-    lse_ref[...] = top + jnp.log2(jnp.sum(jnp.exp2(every - top[None]), axis=0))
-    mine = in_ref[:, pl.ds(32 + me, 1), :]
-    share = jnp.exp2(mine - lse_ref[pl.ds(me, 1), :][None])
+    lse = top + jnp.log2(jnp.sum(jnp.exp2(every - top[None]), axis=0))
+    share = jnp.exp2(every - lse[None])[:, :1, :]
     value = jnp.sum(in_ref[:, :32, :] * share, axis=0)
     for c in range(out_ref.shape[0]):
-        out_ref[c] = value
-
-
-def plan_kernel(scale, total_count, x_ref, y_ref, h_ref, lse_ref, out_ref, g_ref, keys, queries, means):
+        out_ref[c, :32, :] = value
+        out_ref[c, 32:, :] = lse
+
+
+def plan_kernel(scale, total_count, x_ref, y_ref, h_ref, in_ref, out_ref, g_ref, inv_ref, keys, queries, means):
     y = y_ref[...]
-    lse = jnp.concatenate([lse_ref[c : c + 1, :] for c in range(lse_ref.shape[0])], axis=1)
+    lse = jnp.concatenate([in_ref[c, 32:33, :] for c in range(in_ref.shape[0])], axis=1)
     y_sq = jnp.sum(y * y, axis=0, keepdims=True)
     g_ref[...] = (EPS / LOG2E) * (scale * y_sq - math.log2(total_count) - lse)
     keys[...] = key_stack(y, -lse).T
     chunks = x_ref.shape[0]
     queries[...] = query_stack(chunk_row(x_ref, chunks) * (2.0 * scale), h_ref[...])
     means[...] = mean_rows(y)
-
-    def step(at, carry):
-        q = queries[:, pl.ds(pl.multiple_of(at * TILE, TILE), TILE)]
+    for c in range(in_ref.shape[0]):
+        inv_ref[:, c * LANES : (c + 1) * LANES] = in_ref[c, :32, :]
+
+    for at in range(queries.shape[1] // TILE):
+        q = queries[:, at * TILE : (at + 1) * TILE]
         sums = None
-        for k in range(keys.shape[0] // TILE):
-            e = jnp.exp2(dot(keys[k * TILE : (k + 1) * TILE, :], q))
+        for k in range(keys.shape[0] // BLOCK):
+            e = jnp.exp2(dot(keys[k * BLOCK : (k + 1) * BLOCK, :], q))
             sums = weighted(e, means, k, sums)
         for c in range(TILE // LANES):
             cut = slice(c * LANES, (c + 1) * LANES)
             out_ref[at * (TILE // LANES) + c, :32, :] = sums[0][:32, cut] + sums[1][:, cut]
             out_ref[at * (TILE // LANES) + c, 32:, :] = sums[0][32:40, cut]
-        return carry
-
-    lax.fori_loop(0, queries.shape[1] // TILE, step, 0)
-
-
-def finish_kernel(in_ref, inv_ref, out_ref, inv_out_ref):
+
+
+def finish_kernel(in_ref, out_ref):
     sums = jnp.sum(in_ref[...], axis=0)
     out_ref[...] = sums[:32] / sums[32:33]
-    for c in range(inv_ref.shape[0]):
-        inv_out_ref[:, c * LANES : (c + 1) * LANES] = inv_ref[c]
 
 
 def call(body, outs, scratch, flops, *args):
@@ -248,28 +237,28 @@
     stats = lax.all_to_all(stats, "col", 0, 0)
     partial, f, h = call(
         functools.partial(backward_kernel, scale, target_count),
-        [(rows, width + rows, m // rows), (1, n), (1, n)],
-        [keys, queries, scores, means, pltpu.VMEM((rows, m // rows), F32)],
+        [(rows, width + 8, m // rows), (1, n), (1, n)],
+        [keys, queries, scores, means],
         2 * flops,
         x,
         target_points,
         stats,
     )
     partial = lax.all_to_all(partial, "row", 0, 0)
-    inverse, lse = call(reduce_kernel, [(rows, width, m // rows), (rows, m // rows)], [], 1 << 20, partial)
-    inverse = lax.all_to_all(inverse, "row", 0, 0)
-    plan, g = call(
+    (both,) = call(reduce_kernel, [(rows, width + 8, m // rows)], [], 1 << 20, partial)
+    both = lax.all_to_all(both, "row", 0, 0)
+    plan, g, inverse_map = call(
         functools.partial(plan_kernel, scale, source_count),
-        [(cols, width + 8, own), (1, m)],
+        [(cols, width + 8, own), (1, m), (width, m)],
         [keys, queries, means],
         2 * flops,
         x,
         target_points,
         h,
-        lse,
+        both,
     )
     plan = lax.all_to_all(plan, "col", 0, 0)
-    transport_map, inverse_map = call(finish_kernel, [(width, own), (width, m)], [], 1 << 20, plan, inverse)
+    (transport_map,) = call(finish_kernel, [(width, own)], [], 1 << 20, plan)
     return f.reshape(n), g.reshape(m), transport_map, inverse_map
 
 

time: 113 us -> 99 us (0.88)
  Pallas kernels: 31.5 us -> 17.1 us
  blocking collectives: 78.6 us -> 80.2 us
    pallas_call x5, Pallas kernels: 31.5 us -> 17.1 us  [call(): pl.pallas_call(body, out_shape=[jax.ShapeDtypeStruct(s, F32) for s in out...]
    all_to_all x1, blocking collectives: 15.8 us -> 17.4 us  [local(): plan = lax.all_to_all(plan, 'col', 0, 0)]
    all_to_all x1, blocking collectives: 21 us -> 19.4 us  [local(): partial = lax.all_to_all(partial, 'row', 0, 0)]
    all_to_all x1, blocking collectives: 12.7 us -> 14.2 us  [local(): both = lax.all_to_all(both, 'row', 0, 0)]
where the time goes in v2:
time: 99 us; the launch traced here: 98.7 us
  blocking collectives  80.2 us (81%)
  Pallas kernels  17.1 us (17%)
    all_to_all x1, blocking collectives, local(): partial = lax.all_to_all(partial, 'row', 0, 0)  19.4 us
    all_to_all x1, blocking collectives, local(): plan = lax.all_to_all(plan, 'col', 0, 0)  17.4 us
    pallas_call x5, Pallas kernels, call(): pl.pallas_call(body, out_shape=[jax.ShapeDtypeStruct(s, F32) for s in out...  17.1 us
    all_to_all x1, blocking collectives, local(): lax.all_to_all(jnp.broadcast_to(source_points, (cols, width, own)), 'col'...  17 us
    all_to_all x1, blocking collectives, local(): both = lax.all_to_all(both, 'row', 0, 0)  14.2 us
    all_to_all x1, blocking collectives, local(): stats = lax.all_to_all(stats, 'col', 0, 0)  12.1 us

profile of v2, /device:TPU:1, one launch (start us, length us, event | category | flops | bytes accessed | tf_op | source)
XLA Modules:
  0.0 98.7 jit_solution(7740368891354501282)
XLA Ops:
  0.6 0.7 broadcast_in_dim.3
  1.4 0.0 copy-start
  1.4 0.0 copy-start.1
  1.4 17.0 %all_to_all.25.x_ref = f32[16,32,128]{2,1,0:T(8,128)S(1)} all-to-all(f32[16,32,128]{2,1,0:T(8,128)S(1)} %broadcast_in_dim.3), channel_id=1, replica_groups=mesh['row'=16,'col'=16] {'col'}, dimensions={0} | all-to-all | bytes 524288 | tf_op jit(solution)/shard_map/all_to_all | solution.py:227
  18.4 0.0 copy-done
  18.4 0.0 copy-done.1
  18.4 3.9 %shard_map.66 = f32[16,2,2048]{2,1,0:T(2,128)S(1)} custom-call(f32[16,32,128]{2,1,0:T(8,128)S(1)} %all_to_all.25.x_ref, f32[32,2048]{1,0:T(8,128)S(1)} %copy-done, f32[1,2048]{1,0:T(1,128)S(1)} %bitcast.3), custom_call_target="tpu_custom_call" | custom-call | flops 2147483648 | bytes 1048576 | tf_op jit(solution)/shard_map/pallas_call | solution.py:203
  22.4 12.1 %all_to_all.26.stats_ref = f32[16,2,2048]{2,1,0:T(2,128)S(1)} all-to-all(f32[16,2,2048]{2,1,0:T(2,128)S(1)} %shard_map.66), channel_id=1, replica_groups=mesh['row'=16,'col'=16] {'col'}, dimensions={0} | all-to-all | bytes 524288 | tf_op jit(solution)/shard_map/all_to_all | solution.py:237
  34.5 7.0 %shard_map.67 = (f32[16,40,128]{2,1,0:T(8,128)S(1)}, f32[1,2048]{1,0:T(1,128)}, f32[1,2048]{1,0:T(1,128)S(1)}) custom-call(f32[16,32,128]{2,1,0:T(8,128)S(1)} %all_to_all.25.x_ref, f32[32,2048]{1,0:T(8,128)S(1)} %copy-done, f32[16,2,2048]{2,1,0:T(2,128)S(1)} %all_to_all.26.stats_ref), custom_call_target="tpu_custom_call" | custom-call | flops 4294967296 | bytes 1048576 | tf_op jit(solution)/shard_map/pallas_call | solution.py:203
  41.5 19.4 %all_to_all.27.in_ref = f32[16,40,128]{2,1,0:T(8,128)S(1)} all-to-all(f32[16,40,128]{2,1,0:T(8,128)S(1)} %get-tuple-element.12), channel_id=1, replica_groups=mesh['row'=16,'col'=16] {'row'}, dimensions={0} | all-to-all | bytes 655360 | tf_op jit(solution)/shard_map/all_to_all | solution.py:247
  60.9 0.1 shard_map.68
  61.0 14.2 %all_to_all.28.in_ref = f32[16,40,128]{2,1,0:T(8,128)S(1)} all-to-all(f32[16,40,128]{2,1,0:T(8,128)S(1)} %shard_map.68), channel_id=1, replica_groups=mesh['row'=16,'col'=16] {'row'}, dimensions={0} | all-to-all | bytes 655360 | tf_op jit(solution)/shard_map/all_to_all | solution.py:249
  75.1 5.5 %shard_map.69 = (f32[16,40,128]{2,1,0:T(8,128)S(1)}, f32[1,2048]{1,0:T(1,128)}, f32[32,2048]{1,0:T(8,128)}) custom-call(f32[16,32,128]{2,1,0:T(8,128)S(1)} %all_to_all.25.x_ref, f32[32,2048]{1,0:T(8,128)S(1)} %copy-done, f32[1,2048]{1,0:T(1,128)S(1)} %get-tuple-element.11.h_ref, f32[16,40,128]{2,1,0:T(8,128)S(1)} %all_to_all.28.in_ref), custom_call_target="tpu_custom_call" | custom-call | flops 4294967296 | bytes 1048576 | tf_op jit(solution)/shard_map/pallas_call | solution.py:203
  80.6 17.4 %all_to_all.29.in_ref = f32[16,40,128]{2,1,0:T(8,128)S(1)} all-to-all(f32[16,40,128]{2,1,0:T(8,128)S(1)} %get-tuple-element.14), channel_id=1, replica_groups=mesh['row'=16,'col'=16] {'col'}, dimensions={0} | all-to-all | bytes 655360 | tf_op jit(solution)/shard_map/all_to_all | solution.py:260
  98.0 0.6 shard_map.70
Async XLA Ops:
  1.4 17.1 %copy-start = (f32[32,2048]{1,0:T(8,128)S(1)}, f32[32,2048]{1,0:T(8,128)}, u32[]{:S(2)}) copy-start(f32[32,2048]{1,0:T(8,128)} %y_ref.5) | copy-start | bytes 786436
  1.4 17.1 %copy-start.1 = (f32[2048]{0:T(1024)S(1)}, f32[2048]{0:T(1024)}, u32[]{:S(2)}) copy-start(f32[2048]{0:T(1024)} %param.5) | copy-start | bytes 24580

commit v3 on v2

--- a/solution.py
+++ b/solution.py
@@ -127,7 +127,7 @@
     pipelined(queries.shape[1] // TILE, first, second)
 
 
-def backward_kernel(scale, total_count, x_ref, y_ref, stats_ref, out_ref, f_ref, h_ref, keys, queries, scores, means):
+def backward_kernel(scale, total_count, x_ref, y_ref, stats_ref, out_ref, f_ref, h_ref, keys, queries, scores, means, lse):
     chunks = x_ref.shape[0]
     x = chunk_row(x_ref, chunks)
     peaks = stats_ref[:, 0, :]
@@ -150,37 +150,40 @@
             sums = weighted(e, means, k, sums)
         total = sums[0][32:33]
         mean = (sums[0][:32] + sums[1]) / total
-        value = jnp.broadcast_to(peak + jnp.log2(total), (8, TILE))
+        value = peak + jnp.log2(total)
         for c in range(TILE // LANES):
             cut = slice(c * LANES, (c + 1) * LANES)
-            out_ref[at * (TILE // LANES) + c, :32, :] = mean[:, cut]
-            out_ref[at * (TILE // LANES) + c, 32:, :] = value[:, cut]
+            to = at * (TILE // LANES) + c
+            out_ref[to, :32, :] = mean[:, cut]
+            lse[to : to + 1, :] = value[:, cut]
 
     pipelined(queries.shape[1] // TILE, first, second)
-
-
-def reduce_kernel(in_ref, out_ref):
+    rows = lse[...]
+    for c in range(out_ref.shape[0]):
+        out_ref[c, 32:, :] = rows
+
+
+def reduce_kernel(in_ref, out_ref, lse_ref):
+    me = lax.axis_index("row")
     every = in_ref[:, 32:, :]
     top = jnp.max(every, axis=0)
-    lse = top + jnp.log2(jnp.sum(jnp.exp2(every - top[None]), axis=0))
-    share = jnp.exp2(every - lse[None])[:, :1, :]
+    lse_ref[...] = top + jnp.log2(jnp.sum(jnp.exp2(every - top[None]), axis=0))
+    mine = in_ref[:, pl.ds(32 + me, 1), :]
+    share = jnp.exp2(mine - lse_ref[pl.ds(me, 1), :][None])
     value = jnp.sum(in_ref[:, :32, :] * share, axis=0)
     for c in range(out_ref.shape[0]):
-        out_ref[c, :32, :] = value
-        out_ref[c, 32:, :] = lse
-
-
-def plan_kernel(scale, total_count, x_ref, y_ref, h_ref, in_ref, out_ref, g_ref, inv_ref, keys, queries, means):
+        out_ref[c] = value
+
+
+def plan_kernel(scale, total_count, x_ref, y_ref, h_ref, lse_ref, out_ref, g_ref, keys, queries, means):
     y = y_ref[...]
-    lse = jnp.concatenate([in_ref[c, 32:33, :] for c in range(in_ref.shape[0])], axis=1)
+    lse = jnp.concatenate([lse_ref[c : c + 1, :] for c in range(lse_ref.shape[0])], axis=1)
     y_sq = jnp.sum(y * y, axis=0, keepdims=True)
     g_ref[...] = (EPS / LOG2E) * (scale * y_sq - math.log2(total_count) - lse)
     keys[...] = key_stack(y, -lse).T
     chunks = x_ref.shape[0]
     queries[...] = query_stack(chunk_row(x_ref, chunks) * (2.0 * scale), h_ref[...])
     means[...] = mean_rows(y)
-    for c in range(in_ref.shape[0]):
-        inv_ref[:, c * LANES : (c + 1) * LANES] = in_ref[c, :32, :]
 
     for at in range(queries.shape[1] // TILE):
         q = queries[:, at * TILE : (at + 1) * TILE]
@@ -194,9 +197,11 @@
             out_ref[at * (TILE // LANES) + c, 32:, :] = sums[0][32:40, cut]
 
 
-def finish_kernel(in_ref, out_ref):
+def finish_kernel(in_ref, inv_ref, out_ref, inv_out_ref):
     sums = jnp.sum(in_ref[...], axis=0)
     out_ref[...] = sums[:32] / sums[32:33]
+    for c in range(inv_ref.shape[0]):
+        inv_out_ref[:, c * LANES : (c + 1) * LANES] = inv_ref[c]
 
 
 def call(body, outs, scratch, flops, *args):
@@ -237,28 +242,29 @@
     stats = lax.all_to_all(stats, "col", 0, 0)
     partial, f, h = call(
         functools.partial(backward_kernel, scale, target_count),
-        [(rows, width + 8, m // rows), (1, n), (1, n)],
-        [keys, queries, scores, means],
+        [(rows, width + rows, m // rows), (1, n), (1, n)],
+        [keys, queries, scores, means, pltpu.VMEM((rows, m // rows), F32)],
         2 * flops,
         x,
         target_points,
         stats,
     )
     partial = lax.all_to_all(partial, "row", 0, 0)
-    (both,) = call(reduce_kernel, [(rows, width + 8, m // rows)], [], 1 << 20, partial)
-    both = lax.all_to_all(both, "row", 0, 0)
-    plan, g, inverse_map = call(
+    inverse, lse = call(reduce_kernel, [(rows, width, m // rows), (rows, m // rows)], [], 1 << 20, partial)
+    inverse = lax.all_to_all(inverse, "row", 0, 0)
+    plan, g = call(
         functools.partial(plan_kernel, scale, source_count),
-        [(cols, width + 8, own), (1, m), (width, m)],
+        [(cols, width + 8, own), (1, m)],
         [keys, queries, means],
         2 * flops,
         x,
         target_points,
         h,
-        both,
+        lse,
     )
+    plan, inverse = lax.optimization_barrier((plan, inverse))
     plan = lax.all_to_all(plan, "col", 0, 0)
-    (transport_map,) = call(finish_kernel, [(width, own)], [], 1 << 20, plan)
+    transport_map, inverse_map = call(finish_kernel, [(width, own), (width, m)], [], 1 << 20, plan, inverse)
     return f.reshape(n), g.reshape(m), transport_map, inverse_map
 
 

time: 99 us -> 95 us (0.960)
  blocking collectives: 80.2 us -> 67 us
  waiting for transfers between devices: 0 us -> 4.25 us
  starting transfers between devices: 0 us -> 4.05 us
    all_to_all x1 -> x0, blocking collectives: 14.2 us -> none  [local(): both = lax.all_to_all(both, 'row', 0, 0)]
    all_to_all x0 -> x1, waiting for transfers between devices: none -> 4.25 us  [local(): inverse = lax.all_to_all(inverse, 'row', 0, 0)]
    all_to_all x0 -> x1, starting transfers between devices: none -> 4.05 us  [local(): inverse = lax.all_to_all(inverse, 'row', 0, 0)]
    all_to_all x1, blocking collectives: 19.4 us -> 21 us  [local(): partial = lax.all_to_all(partial, 'row', 0, 0)]
  transfers between devices with their start and end apart: 0 -> 1, of which waited for: 0 -> 1; matrix products, arithmetic and copies ran while one was open for 0% -> 0% of each run, Pallas kernels for 0% -> 6%
where the time goes in v3:
time: 95 us; the launch traced here: 94.6 us
  blocking collectives  67 us (71%)
  Pallas kernels  17.8 us (19%)
  waiting for transfers between devices  4.25 us (4%)
  starting transfers between devices  4.05 us (4%)
    all_to_all x1, blocking collectives, local(): partial = lax.all_to_all(partial, 'row', 0, 0)  21 us
    pallas_call x5, Pallas kernels, call(): pl.pallas_call(body, out_shape=[jax.ShapeDtypeStruct(s, F32) for s in out...  17.8 us
    all_to_all x1, blocking collectives, local(): lax.all_to_all(jnp.broadcast_to(source_points, (cols, width, own)), 'col'...  17 us
    all_to_all x1, blocking collectives, local(): plan = lax.all_to_all(plan, 'col', 0, 0)  16.9 us
    all_to_all x1, blocking collectives, local(): stats = lax.all_to_all(stats, 'col', 0, 0)  12.1 us
    all_to_all x1, waiting for transfers between devices, local(): inverse = lax.all_to_all(inverse, 'row', 0, 0)  4.25 us
    all_to_all x1, starting transfers between devices, local(): inverse = lax.all_to_all(inverse, 'row', 0, 0)  4.05 us
  transfers between devices with their start and end apart: 1, of which 1 were waited for; matrix products, arithmetic and copies ran while one was open for 0% of the time, Pallas kernels for 6%

profile of v3, /device:TPU:1, one launch (start us, length us, event | category | flops | bytes accessed | tf_op | source)
XLA Modules:
  0.0 94.6 jit_solution(11209285206198993882)
XLA Ops:
  0.6 0.7 broadcast_in_dim.3
  1.4 0.0 copy-start
  1.4 0.0 copy-start.1
  1.4 17.0 %all_to_all.25.x_ref = f32[16,32,128]{2,1,0:T(8,128)S(1)} all-to-all(f32[16,32,128]{2,1,0:T(8,128)S(1)} %broadcast_in_dim.3), channel_id=1, replica_groups=mesh['row'=16,'col'=16] {'col'}, dimensions={0} | all-to-all | bytes 524288 | tf_op jit(solution)/shard_map/all_to_all | solution.py:232
  18.4 0.0 copy-done
  18.4 0.0 copy-done.1
  18.4 3.9 %shard_map.66 = f32[16,2,2048]{2,1,0:T(2,128)S(1)} custom-call(f32[16,32,128]{2,1,0:T(8,128)S(1)} %all_to_all.25.x_ref, f32[32,2048]{1,0:T(8,128)S(1)} %copy-done, f32[1,2048]{1,0:T(1,128)S(1)} %bitcast.3), custom_call_target="tpu_custom_call" | custom-call | flops 2147483648 | bytes 1048576 | tf_op jit(solution)/shard_map/pallas_call | solution.py:208
  22.4 12.1 %all_to_all.26.stats_ref = f32[16,2,2048]{2,1,0:T(2,128)S(1)} all-to-all(f32[16,2,2048]{2,1,0:T(2,128)S(1)} %shard_map.66), channel_id=1, replica_groups=mesh['row'=16,'col'=16] {'col'}, dimensions={0} | all-to-all | bytes 524288 | tf_op jit(solution)/shard_map/all_to_all | solution.py:242
  34.5 7.0 %shard_map.67 = (f32[16,48,128]{2,1,0:T(8,128)S(1)}, f32[1,2048]{1,0:T(1,128)}, f32[1,2048]{1,0:T(1,128)S(1)}) custom-call(f32[16,32,128]{2,1,0:T(8,128)S(1)} %all_to_all.25.x_ref, f32[32,2048]{1,0:T(8,128)S(1)} %copy-done, f32[16,2,2048]{2,1,0:T(2,128)S(1)} %all_to_all.26.stats_ref), custom_call_target="tpu_custom_call" | custom-call | flops 4294967296 | bytes 1048576 | tf_op jit(solution)/shard_map/pallas_call | solution.py:208
  41.5 21.0 %all_to_all.27.in_ref = f32[16,48,128]{2,1,0:T(8,128)S(1)} all-to-all(f32[16,48,128]{2,1,0:T(8,128)S(1)} %get-tuple-element.17), channel_id=1, replica_groups=mesh['row'=16,'col'=16] {'row'}, dimensions={0} | all-to-all | bytes 786432 | tf_op jit(solution)/shard_map/all_to_all | solution.py:252
  62.5 0.8 shard_map.68
  63.3 4.1 %all-to-all-start.3 = ((f32[16,32,128]{2,1,0:T(8,128)}), f32[16,32,128]{2,1,0:T(8,128)S(1)}, u32[]{:S(2)}, u32[]{:S(2)}) async-start(f32[16,32,128]{2,1,0:T(8,128)} %get-tuple-element.21), calls=%async_computation.3 | async-start | bytes 524288 | tf_op jit(solution)/shard_map/all_to_all | solution.py:254
  67.3 5.4 %shard_map.69 = (f32[16,40,128]{2,1,0:T(8,128)S(1)}, f32[1,2048]{1,0:T(1,128)}) custom-call(f32[16,32,128]{2,1,0:T(8,128)S(1)} %all_to_all.25.x_ref, f32[32,2048]{1,0:T(8,128)S(1)} %copy-done, f32[1,2048]{1,0:T(1,128)S(1)} %get-tuple-element.16.h_ref, f32[16,128]{1,0:T(8,128)S(1)} %get-tuple-element.18.lse_ref), custom_call_target="tpu_custom_call" | custom-call | flops 4294967296 | bytes 1048576 | tf_op jit(solution)/shard_map/pallas_call | solution.py:208
  72.7 4.2 %all-to-all-done.3.inv_ref = f32[16,32,128]{2,1,0:T(8,128)S(1)} async-done(((f32[16,32,128]{2,1,0:T(8,128)}), f32[16,32,128]{2,1,0:T(8,128)S(1)}, u32[]{:S(2)}, u32[]{:S(2)}) %all-to-all-start.3) | async-done | bytes 262176 | tf_op jit(solution)/shard_map/all_to_all | solution.py:254
  76.9 16.9 %all_to_all.28.in_ref = f32[16,40,128]{2,1,0:T(8,128)S(1)} all-to-all(f32[16,40,128]{2,1,0:T(8,128)S(1)} %get-tuple-element.22), channel_id=1, replica_groups=mesh['row'=16,'col'=16] {'col'}, dimensions={0} | all-to-all | bytes 655360 | tf_op jit(solution)/shard_map/all_to_all | solution.py:266
  93.8 0.7 shard_map.70
Async XLA Ops:
  1.4 17.1 %copy-start = (f32[32,2048]{1,0:T(8,128)S(1)}, f32[32,2048]{1,0:T(8,128)}, u32[]{:S(2)}) copy-start(f32[32,2048]{1,0:T(8,128)} %y_ref.5) | copy-start | bytes 786436
  1.4 17.1 %copy-start.1 = (f32[2048]{0:T(1024)S(1)}, f32[2048]{0:T(1024)}, u32[]{:S(2)}) copy-start(f32[2048]{0:T(1024)} %param.5) | copy-start | bytes 24580
  63.3 13.7 %all-to-all-start.3 = ((f32[16,32,128]{2,1,0:T(8,128)}), f32[16,32,128]{2,1,0:T(8,128)S(1)}, u32[]{:S(2)}, u32[]{:S(2)}) async-start(f32[16,32,128]{2,1,0:T(8,128)} %get-tuple-element.21), calls=%async_computation.3 | async-start | bytes 524288 | tf_op jit(solution)/shard_map/all_to_all | solution.py:254

commit v4 on v3

--- a/solution.py
+++ b/solution.py
@@ -1,5 +1,6 @@
 import functools
 import math
+import operator
 
 import jax
 import jax.numpy as jnp
@@ -14,6 +15,8 @@
 LANES = 128
 TILE = 256
 BLOCK = 512
+SMALL = 256
+HOPS = (1, -2, 3)
 LOG2E = math.log2(math.e)
 VMEM_LIMIT = 48 * 1024 * 1024
 
@@ -52,11 +55,11 @@
 
 
 def mean_rows(points):
-    a, b, c = split(points, 3)
+    a, b = split(points, 2)
     ones = weight_rows(None, jnp.zeros((1, points.shape[1]), F32))
     keep = lax.broadcasted_iota(jnp.int32, ones.shape, 0) == 0
     ones = jnp.where(keep, ones.astype(F32), 0.0).astype(BF16)
-    return jnp.concatenate([a, ones, b, c], axis=0)
+    return jnp.concatenate([b, a, ones], axis=0)
 
 
 def dot(a, b):
@@ -72,37 +75,19 @@
     return jnp.max(scores.reshape(rows // 8, 8, cols), axis=0)
 
 
-def scores_tile(keys, queries, scores, at):
-    q = queries[:, at * TILE : (at + 1) * TILE]
-    peak = None
-    for k in range(keys.shape[0] // BLOCK):
-        s = dot(keys[k * BLOCK : (k + 1) * BLOCK, :], q)
-        scores[at % 2, k * BLOCK : (k + 1) * BLOCK, :] = s
-        p = peak8(s)
-        peak = p if peak is None else jnp.maximum(peak, p)
-    return jnp.max(peak, axis=0, keepdims=True)
-
-
-def weighted(expos, means, k, sums):
+def weighted(expos, means, k):
     high = expos.astype(BF16)
     low = (expos - high.astype(F32)).astype(BF16)
     m = means[:, k * BLOCK : (k + 1) * BLOCK]
-    full = dot(m, high)
-    rest = dot(m[:80], low)
-    part = full[:48] + rest[:48]
-    tail = full[48:80] + full[80:112] + rest[48:80]
-    return (part, tail) if sums is None else (sums[0] + part, sums[1] + tail)
-
-
-def pipelined(steps, first, second):
-    peak = first(0)
-    for at in range(steps):
-        later = first(at + 1) if at + 1 < steps else None
-        second(at, peak)
-        peak = later
-
-
-def forward_kernel(scale, x_ref, y_ref, g_ref, out_ref, keys, queries, scores):
+    return [dot(m, high), dot(m[32:], low)]
+
+
+def joined(sums):
+    full, rest = sums
+    return full[:32] + full[32:64] + rest[:32], full[64:72] + rest[32:40]
+
+
+def forward_kernel(scale, x_ref, y_ref, g_ref, out_ref, keys, queries):
     count = y_ref.shape[1]
     y = y_ref[...]
     weight = g_ref[...] * (LOG2E / EPS) - scale * jnp.sum(y * y, axis=0, keepdims=True)
@@ -110,24 +95,24 @@
     chunks = x_ref.shape[0]
     queries[...] = query_stack(chunk_row(x_ref, chunks) * (2.0 * scale), None)
 
-    def first(at):
-        return scores_tile(keys, queries, scores, at)
-
-    def second(at, peak):
-        total = None
-        for k in range(count // BLOCK):
-            e = jnp.exp2(scores[at % 2, k * BLOCK : (k + 1) * BLOCK, :] - peak)
-            t = jnp.sum(e.reshape(BLOCK // 8, 8, TILE), axis=0)
-            total = t if total is None else total + t
-        total = jnp.sum(total, axis=0, keepdims=True)
-        pair = jnp.concatenate([peak, total], axis=0)
+    for at in range(queries.shape[1] // TILE):
+        q = queries[:, at * TILE : (at + 1) * TILE]
+        peak, total = None, None
+        for k in range(count // SMALL):
+            s = dot(keys[k * SMALL : (k + 1) * SMALL, :], q).reshape(SMALL // 8, 8, TILE)
+            top = jnp.max(s, axis=0)
+            later = top if peak is None else jnp.maximum(peak, top)
+            t = jnp.sum(jnp.exp2(s - later[None]), axis=0)
+            total = t if total is None else total * jnp.exp2(peak - later) + t
+            peak = later
+        top = jnp.max(peak, axis=0, keepdims=True)
+        total = jnp.sum(total * jnp.exp2(peak - top), axis=0, keepdims=True)
+        pair = jnp.concatenate([top, total], axis=0)
         for c in range(out_ref.shape[0]):
             out_ref[c, :, at * TILE : (at + 1) * TILE] = pair
 
-    pipelined(queries.shape[1] // TILE, first, second)
-
-
-def backward_kernel(scale, total_count, x_ref, y_ref, stats_ref, out_ref, f_ref, h_ref, keys, queries, scores, means, lse):
+
+def backward_kernel(scale, total_count, x_ref, y_ref, stats_ref, out_ref, f_ref, h_ref, keys, queries, means, lse):
     chunks = x_ref.shape[0]
     x = chunk_row(x_ref, chunks)
     peaks = stats_ref[:, 0, :]
@@ -140,16 +125,22 @@
     queries[...] = query_stack(y_ref[...] * (2.0 * scale), None)
     means[...] = mean_rows(x)
 
-    def first(at):
-        return scores_tile(keys, queries, scores, at)
-
-    def second(at, peak):
-        sums = None
+    for at in range(queries.shape[1] // TILE):
+        q = queries[:, at * TILE : (at + 1) * TILE]
+        peak, sums = None, None
         for k in range(keys.shape[0] // BLOCK):
-            e = jnp.exp2(scores[at % 2, k * BLOCK : (k + 1) * BLOCK, :] - peak)
-            sums = weighted(e, means, k, sums)
-        total = sums[0][32:33]
-        mean = (sums[0][:32] + sums[1]) / total
+            s = dot(keys[k * BLOCK : (k + 1) * BLOCK, :], q)
+            top = jnp.max(peak8(s), axis=0, keepdims=True)
+            later = top if peak is None else jnp.maximum(peak, top)
+            part = weighted(jnp.exp2(s - later), means, k)
+            if sums is None:
+                sums = part
+            else:
+                factor = jnp.exp2(peak - later)
+                sums = [old * factor + new for old, new in zip(sums, part)]
+            peak = later
+        mean, total = joined(sums)
+        mean, total = mean / total[:1], total[:1]
         value = peak + jnp.log2(total)
         for c in range(TILE // LANES):
             cut = slice(c * LANES, (c + 1) * LANES)
@@ -157,7 +148,6 @@
             out_ref[to, :32, :] = mean[:, cut]
             lse[to : to + 1, :] = value[:, cut]
 
-    pipelined(queries.shape[1] // TILE, first, second)
     rows = lse[...]
     for c in range(out_ref.shape[0]):
         out_ref[c, 32:, :] = rows
@@ -170,9 +160,7 @@
     lse_ref[...] = top + jnp.log2(jnp.sum(jnp.exp2(every - top[None]), axis=0))
     mine = in_ref[:, pl.ds(32 + me, 1), :]
     share = jnp.exp2(mine - lse_ref[pl.ds(me, 1), :][None])
-    value = jnp.sum(in_ref[:, :32, :] * share, axis=0)
-    for c in range(out_ref.shape[0]):
-        out_ref[c] = value
+    out_ref[...] = jnp.sum(in_ref[:, :32, :] * share, axis=0)
 
 
 def plan_kernel(scale, total_count, x_ref, y_ref, h_ref, lse_ref, out_ref, g_ref, keys, queries, means):
@@ -190,18 +178,38 @@
         sums = None
         for k in range(keys.shape[0] // BLOCK):
             e = jnp.exp2(dot(keys[k * BLOCK : (k + 1) * BLOCK, :], q))
-            sums = weighted(e, means, k, sums)
+            part = weighted(e, means, k)
+            sums = part if sums is None else [old + new for old, new in zip(sums, part)]
+        mean, total = joined(sums)
         for c in range(TILE // LANES):
             cut = slice(c * LANES, (c + 1) * LANES)
-            out_ref[at * (TILE // LANES) + c, :32, :] = sums[0][:32, cut] + sums[1][:, cut]
-            out_ref[at * (TILE // LANES) + c, 32:, :] = sums[0][32:40, cut]
-
-
-def finish_kernel(in_ref, inv_ref, out_ref, inv_out_ref):
+            out_ref[at * (TILE // LANES) + c, :32, :] = mean[:, cut]
+            out_ref[at * (TILE // LANES) + c, 32:, :] = total[:, cut]
+
+
+def outward(hop, z):
+    return z + hop if z % 2 == 1 else z - hop
+
+
+def from_rows(value, rows, level, side):
+    levels = rows // 2
+    return lax.ppermute(value, "row", [(level(r // 2) % levels * 2 + (r % 2 ^ side), r) for r in range(rows)])
+
+
+def finish_kernel(in_ref, *refs):
+    pieces, (out_ref, inv_ref) = refs[:-2], refs[-2:]
     sums = jnp.sum(in_ref[...], axis=0)
     out_ref[...] = sums[:32] / sums[32:33]
-    for c in range(inv_ref.shape[0]):
-        inv_out_ref[:, c * LANES : (c + 1) * LANES] = inv_ref[c]
+    me = lax.axis_index("row")
+    levels = inv_ref.shape[1] // LANES // 2
+    level, side = me // 2, me % 2
+    sign = 2 * (level % 2) - 1
+    for ref, hop in zip(pieces, (0,) + HOPS):
+        source = lax.rem(level + sign * hop + levels, levels)
+        mate = source + 1 - 2 * (source % 2)
+        for at in range(4):
+            chunk = (source if at < 2 else mate) * 2 + (side if at % 2 == 0 else 1 - side)
+            inv_ref[:, pl.ds(pl.multiple_of(chunk * LANES, LANES), LANES)] = ref[at * 32 : (at + 1) * 32, :]
 
 
 def call(body, outs, scratch, flops, *args):
@@ -225,15 +233,14 @@
     depth = 6 * width + 16
     keys = pltpu.VMEM((m, depth), BF16)
     queries = pltpu.VMEM((depth, n), BF16)
-    scores = pltpu.VMEM((2, m, TILE), F32)
-    means = pltpu.VMEM((3 * width + 16, m), BF16)
+    means = pltpu.VMEM((2 * width + 16, m), BF16)
     flops = 2 * n * m * 256
 
     x = lax.all_to_all(jnp.broadcast_to(source_points, (cols, width, own)), "col", 0, 0)
     (stats,) = call(
         functools.partial(forward_kernel, scale),
         [(cols, 2, n)],
-        [keys, queries, scores],
+        [keys, queries],
         flops,
         x,
         target_points,
@@ -243,15 +250,17 @@
     partial, f, h = call(
         functools.partial(backward_kernel, scale, target_count),
         [(rows, width + rows, m // rows), (1, n), (1, n)],
-        [keys, queries, scores, means, pltpu.VMEM((rows, m // rows), F32)],
+        [keys, queries, means, pltpu.VMEM((rows, m // rows), F32)],
         2 * flops,
         x,
         target_points,
         stats,
     )
     partial = lax.all_to_all(partial, "row", 0, 0)
-    inverse, lse = call(reduce_kernel, [(rows, width, m // rows), (rows, m // rows)], [], 1 << 20, partial)
-    inverse = lax.all_to_all(inverse, "row", 0, 0)
+    inverse, lse = call(reduce_kernel, [(width, m // rows), (rows, m // rows)], [], 1 << 20, partial)
+    pieces = [inverse] + [from_rows(inverse, rows, functools.partial(operator.xor, level), side) for level, side in ((0, 1), (1, 0), (1, 1))]
+    four = jnp.concatenate(pieces, axis=0)
+    pieces = [four] + [from_rows(four, rows, functools.partial(outward, hop), 0) for hop in HOPS]
     plan, g = call(
         functools.partial(plan_kernel, scale, source_count),
         [(cols, width + 8, own), (1, m)],
@@ -262,9 +271,8 @@
         h,
         lse,
     )
-    plan, inverse = lax.optimization_barrier((plan, inverse))
     plan = lax.all_to_all(plan, "col", 0, 0)
-    transport_map, inverse_map = call(finish_kernel, [(width, own), (width, m)], [], 1 << 20, plan, inverse)
+    transport_map, inverse_map = call(finish_kernel, [(width, own), (width, m)], [], 1 << 20, plan, *pieces)
     return f.reshape(n), g.reshape(m), transport_map, inverse_map
 
 

time: 95 us -> 88.3 us (0.929)
  blocking collectives: 67 us -> 50.1 us
  starting transfers between devices: 4.05 us -> 13.9 us
  waiting for transfers between devices: 4.25 us -> 5.61 us
  Pallas kernels: 17.8 us -> 16.8 us
    all_to_all x1 -> x0, blocking collectives: 16.9 us -> none  [local(): plan = lax.all_to_all(plan, 'col', 0, 0)]
    ppermute x0 -> x6, starting transfers between devices: none -> 6.25 us  [from_rows(): lax.ppermute(value, 'row', [(level(r // 2) % levels * 2 + (r % 2 ^ side),...]
    ppermute x0 -> x6, waiting for transfers between devices: none -> 5.61 us  [from_rows(): lax.ppermute(value, 'row', [(level(r // 2) % levels * 2 + (r % 2 ^ side),...]
    all_to_all x1, waiting for transfers between devices: 4.25 us -> 0.01 us  [local(): plan = lax.all_to_all(plan, 'col', 0, 0)]
    all_to_all x1, starting transfers between devices: 4.05 us -> 7.66 us  [local(): plan = lax.all_to_all(plan, 'col', 0, 0)]
    pallas_call x5, Pallas kernels: 17.8 us -> 16.8 us  [call(): pl.pallas_call(body, out_shape=[jax.ShapeDtypeStruct(s, F32) for s in out...]
  transfers between devices with their start and end apart: 1 -> 7, of which waited for: 1 -> 2; matrix products, arithmetic and copies ran while one was open for 0% -> 0% of each run, Pallas kernels for 6% -> 7%
where the time goes in v4:
time: 88.3 us; the launch traced here: 88 us
  blocking collectives  50.1 us (57%)
  Pallas kernels  16.8 us (19%)
  starting transfers between devices  13.9 us (16%)
  waiting for transfers between devices  5.61 us (6%)
    all_to_all x1, blocking collectives, local(): partial = lax.all_to_all(partial, 'row', 0, 0)  21 us
    all_to_all x1, blocking collectives, local(): lax.all_to_all(jnp.broadcast_to(source_points, (cols, width, own)), 'col'...  17 us
    pallas_call x5, Pallas kernels, call(): pl.pallas_call(body, out_shape=[jax.ShapeDtypeStruct(s, F32) for s in out...  16.8 us
    all_to_all x1, blocking collectives, local(): stats = lax.all_to_all(stats, 'col', 0, 0)  12.1 us
    all_to_all x1, starting transfers between devices, local(): plan = lax.all_to_all(plan, 'col', 0, 0)  7.66 us
    ppermute x6, starting transfers between devices, from_rows(): lax.ppermute(value, 'row', [(level(r // 2) % levels * 2 + (r % 2 ^ side),...  6.25 us
    ppermute x6, waiting for transfers between devices, from_rows(): lax.ppermute(value, 'row', [(level(r // 2) % levels * 2 + (r % 2 ^ side),...  5.61 us
  transfers between devices with their start and end apart: 7, of which 2 were waited for; matrix products, arithmetic and copies ran while one was open for 0% of the time, Pallas kernels for 7%

profile of v4, /device:TPU:1, one launch (start us, length us, event | category | flops | bytes accessed | tf_op | source)
XLA Modules:
  0.0 88.0 jit_solution(13334883851274893606)
XLA Ops:
  0.6 0.7 broadcast_in_dim.3
  1.4 0.0 copy-start
  1.4 0.0 copy-start.1
  1.4 17.0 %all_to_all.20.x_ref = f32[16,32,128]{2,1,0:T(8,128)S(1)} all-to-all(f32[16,32,128]{2,1,0:T(8,128)S(1)} %broadcast_in_dim.3), channel_id=1, replica_groups=mesh['row'=16,'col'=16] {'col'}, dimensions={0} | all-to-all | bytes 524288 | tf_op jit(solution)/shard_map/all_to_all | solution.py:239
  18.4 0.0 copy-done
  18.4 0.0 copy-done.1
  18.4 3.6 %shard_map.66 = f32[16,2,2048]{2,1,0:T(2,128)S(1)} custom-call(f32[16,32,128]{2,1,0:T(8,128)S(1)} %all_to_all.20.x_ref, f32[32,2048]{1,0:T(8,128)S(1)} %copy-done, f32[1,2048]{1,0:T(1,128)S(1)} %bitcast.3), custom_call_target="tpu_custom_call" | custom-call | flops 2147483648 | bytes 1048576 | tf_op jit(solution)/shard_map/pallas_call | solution.py:216
  22.0 12.1 %all_to_all.21.stats_ref = f32[16,2,2048]{2,1,0:T(2,128)S(1)} all-to-all(f32[16,2,2048]{2,1,0:T(2,128)S(1)} %shard_map.66), channel_id=1, replica_groups=mesh['row'=16,'col'=16] {'col'}, dimensions={0} | all-to-all | bytes 524288 | tf_op jit(solution)/shard_map/all_to_all | solution.py:249
  34.2 6.4 %shard_map.67 = (f32[16,48,128]{2,1,0:T(8,128)S(1)}, f32[1,2048]{1,0:T(1,128)}, f32[1,2048]{1,0:T(1,128)S(1)}) custom-call(f32[16,32,128]{2,1,0:T(8,128)S(1)} %all_to_all.20.x_ref, f32[32,2048]{1,0:T(8,128)S(1)} %copy-done, f32[16,2,2048]{2,1,0:T(2,128)S(1)} %all_to_all.21.stats_ref), custom_call_target="tpu_custom_call" | custom-call | flops 4294967296 | bytes 1048576 | tf_op jit(solution)/shard_map/pallas_call | solution.py:216
  40.5 21.0 %all_to_all.22.in_ref = f32[16,48,128]{2,1,0:T(8,128)S(1)} all-to-all(f32[16,48,128]{2,1,0:T(8,128)S(1)} %get-tuple-element.15), channel_id=1, replica_groups=mesh['row'=16,'col'=16] {'row'}, dimensions={0} | all-to-all | bytes 786432 | tf_op jit(solution)/shard_map/all_to_all | solution.py:259
  61.5 0.1 shard_map.68
  61.6 0.1 collective-permute-start.2
  61.7 1.3 %collective-permute-start.1 = (f32[32,128]{1,0:T(8,128)S(1)}, f32[32,128]{1,0:T(8,128)S(1)}, u32[]{:S(2)}, u32[]{:S(2)}) collective-permute-start(f32[32,128]{1,0:T(8,128)S(1)} %get-tuple-element.19), channel_id=1, source_target_pairs={{32,0},{48,16},{0,32},{16,48},{96,64},{112,80},{64,96},{80,112},{1... | collective-permute-start | bytes 49160 | tf_op jit(solution)/shard_map/ppermute | solution.py:196
  62.9 1.4 %collective-permute-start = (f32[32,128]{1,0:T(8,128)S(1)}, f32[32,128]{1,0:T(8,128)S(1)}, u32[]{:S(2)}, u32[]{:S(2)}) collective-permute-start(f32[32,128]{1,0:T(8,128)S(1)} %get-tuple-element.19), channel_id=1, source_target_pairs={{16,0},{0,16},{48,32},{32,48},{80,64},{64,80},{112,96},{96,112},{1... | collective-permute-start | bytes 49160 | tf_op jit(solution)/shard_map/ppermute | solution.py:196
  64.3 6.0 %shard_map.69 = (f32[16,40,128]{2,1,0:T(8,128)}, f32[1,2048]{1,0:T(1,128)}) custom-call(f32[16,32,128]{2,1,0:T(8,128)S(1)} %all_to_all.20.x_ref, f32[32,2048]{1,0:T(8,128)S(1)} %copy-done, f32[1,2048]{1,0:T(1,128)S(1)} %get-tuple-element.14.h_ref, f32[16,128]{1,0:T(8,128)S(1)} %get-tuple-element.16.lse_ref), custom_call_target="tpu_custom_call" | custom-call | flops 4294967296 | bytes 1048576 | tf_op jit(solution)/shard_map/pallas_call | solution.py:216
  70.3 7.7 %all-to-all-start.3 = ((f32[16,40,128]{2,1,0:T(8,128)}), f32[16,40,128]{2,1,0:T(8,128)S(1)}, u32[]{:S(2)}, u32[]{:S(2)}) async-start(f32[16,40,128]{2,1,0:T(8,128)} %get-tuple-element.18), calls=%async_computation.3 | async-start | bytes 655360 | tf_op jit(solution)/shard_map/all_to_all | solution.py:274
  78.0 0.0 collective-permute-done
  78.0 0.0 collective-permute-done.1
  78.0 0.0 collective-permute-done.2
  78.1 0.2 collective-permute-start.5
  78.2 3.1 %collective-permute-start.4 = (f32[128,128]{1,0:T(8,128)S(1)}, f32[128,128]{1,0:T(8,128)S(1)}, u32[]{:S(2)}, u32[]{:S(2)}) collective-permute-start(f32[128,128]{1,0:T(8,128)S(1)} %constant_dynamic-update-slice_fusion.refs_0_), channel_id=1, source_target_pairs={{64,0},{80,16},{224,32},{240,48},{128,64},{144,80},{32,96},{48,112... | collective-permute-start | bytes 196616 | tf_op jit(solution)/shard_map/ppermute | solution.py:196
  81.3 0.3 collective-permute-start.3
  81.6 3.7 %collective-permute-done.5.refs_3_ = f32[128,128]{1,0:T(8,128)S(1)} collective-permute-done((f32[128,128]{1,0:T(8,128)S(1)}, f32[128,128]{1,0:T(8,128)S(1)}, u32[]{:S(2)}, u32[]{:S(2)}) %collective-permute-start.5) | collective-permute-done | bytes 65568 | tf_op jit(solution)/shard_map/ppermute | solution.py:196
  85.3 0.0 collective-permute-done.4.refs_2_
  85.3 1.9 %collective-permute-done.3.refs_1_ = f32[128,128]{1,0:T(8,128)S(1)} collective-permute-done((f32[128,128]{1,0:T(8,128)S(1)}, f32[128,128]{1,0:T(8,128)S(1)}, u32[]{:S(2)}, u32[]{:S(2)}) %collective-permute-start.3) | collective-permute-done | bytes 65568 | tf_op jit(solution)/shard_map/ppermute | solution.py:196
  87.2 0.0 all-to-all-done.3.in_ref
  87.2 0.8 shard_map.70
  (4 shorter events, 0.0 us)
Async XLA Ops:
  1.4 17.1 %copy-start = (f32[32,2048]{1,0:T(8,128)S(1)}, f32[32,2048]{1,0:T(8,128)}, u32[]{:S(2)}) copy-start(f32[32,2048]{1,0:T(8,128)} %y_ref.5) | copy-start | bytes 786436
  1.4 17.1 %copy-start.1 = (f32[2048]{0:T(1024)S(1)}, f32[2048]{0:T(1024)}, u32[]{:S(2)}) copy-start(f32[2048]{0:T(1024)} %param.5) | copy-start | bytes 24580
  61.6 16.5 %collective-permute-start.2 = (f32[32,128]{1,0:T(8,128)S(1)}, f32[32,128]{1,0:T(8,128)S(1)}, u32[]{:S(2)}, u32[]{:S(2)}) collective-permute-start(f32[32,128]{1,0:T(8,128)S(1)} %get-tuple-element.19), channel_id=1, source_target_pairs={{48,0},{32,16},{16,32},{0,48},{112,64},{96,80},{80,96},{64,112},{1... | collective-permute-start | bytes 49160 | tf_op jit(solution)/shard_map/ppermute | solution.py:196
  61.7 16.4 %collective-permute-start.1 = (f32[32,128]{1,0:T(8,128)S(1)}, f32[32,128]{1,0:T(8,128)S(1)}, u32[]{:S(2)}, u32[]{:S(2)}) collective-permute-start(f32[32,128]{1,0:T(8,128)S(1)} %get-tuple-element.19), channel_id=1, source_target_pairs={{32,0},{48,16},{0,32},{16,48},{96,64},{112,80},{64,96},{80,112},{1... | collective-permute-start | bytes 49160 | tf_op jit(solution)/shard_map/ppermute | solution.py:196
  62.9 15.1 %collective-permute-start = (f32[32,128]{1,0:T(8,128)S(1)}, f32[32,128]{1,0:T(8,128)S(1)}, u32[]{:S(2)}, u32[]{:S(2)}) collective-permute-start(f32[32,128]{1,0:T(8,128)S(1)} %get-tuple-element.19), channel_id=1, source_target_pairs={{16,0},{0,16},{48,32},{32,48},{80,64},{64,80},{112,96},{96,112},{1... | collective-permute-start | bytes 49160 | tf_op jit(solution)/shard_map/ppermute | solution.py:196
  70.3 16.9 %all-to-all-start.3 = ((f32[16,40,128]{2,1,0:T(8,128)}), f32[16,40,128]{2,1,0:T(8,128)S(1)}, u32[]{:S(2)}, u32[]{:S(2)}) async-start(f32[16,40,128]{2,1,0:T(8,128)} %get-tuple-element.18), calls=%async_computation.3 | async-start | bytes 655360 | tf_op jit(solution)/shard_map/all_to_all | solution.py:274
  78.1 7.2 %collective-permute-start.5 = (f32[128,128]{1,0:T(8,128)S(1)}, f32[128,128]{1,0:T(8,128)S(1)}, u32[]{:S(2)}, u32[]{:S(2)}) collective-permute-start(f32[128,128]{1,0:T(8,128)S(1)} %constant_dynamic-update-slice_fusion.refs_0_), channel_id=1, source_target_pairs={{160,0},{176,16},{128,32},{144,48},{224,64},{240,80},{192,96},{208... | collective-permute-start | bytes 196616 | tf_op jit(solution)/shard_map/ppermute | solution.py:196
  78.2 7.1 %collective-permute-start.4 = (f32[128,128]{1,0:T(8,128)S(1)}, f32[128,128]{1,0:T(8,128)S(1)}, u32[]{:S(2)}, u32[]{:S(2)}) collective-permute-start(f32[128,128]{1,0:T(8,128)S(1)} %constant_dynamic-update-slice_fusion.refs_0_), channel_id=1, source_target_pairs={{64,0},{80,16},{224,32},{240,48},{128,64},{144,80},{32,96},{48,112... | collective-permute-start | bytes 196616 | tf_op jit(solution)/shard_map/ppermute | solution.py:196
  81.3 5.9 %collective-permute-start.3 = (f32[128,128]{1,0:T(8,128)S(1)}, f32[128,128]{1,0:T(8,128)S(1)}, u32[]{:S(2)}, u32[]{:S(2)}) collective-permute-start(f32[128,128]{1,0:T(8,128)S(1)} %constant_dynamic-update-slice_fusion.refs_0_), channel_id=1, source_target_pairs={{224,0},{240,16},{64,32},{80,48},{32,64},{48,80},{128,96},{144,112... | collective-permute-start | bytes 196616 | tf_op jit(solution)/shard_map/ppermute | solution.py:196

commit v5 on v4

--- a/solution.py
+++ b/solution.py
@@ -55,11 +55,11 @@
 
 
 def mean_rows(points):
-    a, b = split(points, 2)
+    a, b, c = split(points, 3)
     ones = weight_rows(None, jnp.zeros((1, points.shape[1]), F32))
     keep = lax.broadcasted_iota(jnp.int32, ones.shape, 0) == 0
     ones = jnp.where(keep, ones.astype(F32), 0.0).astype(BF16)
-    return jnp.concatenate([b, a, ones], axis=0)
+    return jnp.concatenate([a, ones, b, c], axis=0)
 
 
 def dot(a, b):
@@ -79,12 +79,13 @@
     high = expos.astype(BF16)
     low = (expos - high.astype(F32)).astype(BF16)
     m = means[:, k * BLOCK : (k + 1) * BLOCK]
-    return [dot(m, high), dot(m[32:], low)]
+    full, rest = dot(m, high), dot(m[:80], low)
+    return [full[:48] + rest[:48], full[48:80] + full[80:112] + rest[48:80]]
 
 
 def joined(sums):
-    full, rest = sums
-    return full[:32] + full[32:64] + rest[:32], full[64:72] + rest[32:40]
+    part, tail = sums
+    return part[:32] + tail, part[32:40]
 
 
 def forward_kernel(scale, x_ref, y_ref, g_ref, out_ref, keys, queries):
@@ -112,7 +113,7 @@
             out_ref[c, :, at * TILE : (at + 1) * TILE] = pair
 
 
-def backward_kernel(scale, total_count, x_ref, y_ref, stats_ref, out_ref, f_ref, h_ref, keys, queries, means, lse):
+def backward_kernel(scale, total_count, x_ref, y_ref, stats_ref, out_ref, h_ref, keys, queries, means, lse):
     chunks = x_ref.shape[0]
     x = chunk_row(x_ref, chunks)
     peaks = stats_ref[:, 0, :]
@@ -120,7 +121,6 @@
     total = jnp.sum(stats_ref[:, 1, :] * jnp.exp2(peaks - top), axis=0, keepdims=True)
     h = -math.log2(total_count) - (top + jnp.log2(total))
     h_ref[...] = h
-    f_ref[...] = (EPS / LOG2E) * (h + scale * jnp.sum(x * x, axis=0, keepdims=True))
     keys[...] = key_stack(x, h).T
     queries[...] = query_stack(y_ref[...] * (2.0 * scale), None)
     means[...] = mean_rows(x)
@@ -163,11 +163,9 @@
     out_ref[...] = jnp.sum(in_ref[:, :32, :] * share, axis=0)
 
 
-def plan_kernel(scale, total_count, x_ref, y_ref, h_ref, lse_ref, out_ref, g_ref, keys, queries, means):
+def plan_kernel(scale, x_ref, y_ref, h_ref, lse_ref, out_ref, keys, queries, means):
     y = y_ref[...]
     lse = jnp.concatenate([lse_ref[c : c + 1, :] for c in range(lse_ref.shape[0])], axis=1)
-    y_sq = jnp.sum(y * y, axis=0, keepdims=True)
-    g_ref[...] = (EPS / LOG2E) * (scale * y_sq - math.log2(total_count) - lse)
     keys[...] = key_stack(y, -lse).T
     chunks = x_ref.shape[0]
     queries[...] = query_stack(chunk_row(x_ref, chunks) * (2.0 * scale), h_ref[...])
@@ -194,6 +192,15 @@
 def from_rows(value, rows, level, side):
     levels = rows // 2
     return lax.ppermute(value, "row", [(level(r // 2) % levels * 2 + (r % 2 ^ side), r) for r in range(rows)])
+
+
+def potentials_kernel(scale, total_count, x_ref, y_ref, h_ref, lse_ref, f_ref, g_ref):
+    x, y = chunk_row(x_ref, x_ref.shape[0]), y_ref[...]
+    lse = jnp.concatenate([lse_ref[c : c + 1, :] for c in range(lse_ref.shape[0])], axis=1)
+    x_sq = jnp.sum(x * x, axis=0, keepdims=True)
+    y_sq = jnp.sum(y * y, axis=0, keepdims=True)
+    f_ref[...] = (EPS / LOG2E) * (h_ref[...] + scale * x_sq)
+    g_ref[...] = (EPS / LOG2E) * (scale * y_sq - math.log2(total_count) - lse)
 
 
 def finish_kernel(in_ref, *refs):
@@ -233,7 +240,7 @@
     depth = 6 * width + 16
     keys = pltpu.VMEM((m, depth), BF16)
     queries = pltpu.VMEM((depth, n), BF16)
-    means = pltpu.VMEM((2 * width + 16, m), BF16)
+    means = pltpu.VMEM((3 * width + 16, m), BF16)
     flops = 2 * n * m * 256
 
     x = lax.all_to_all(jnp.broadcast_to(source_points, (cols, width, own)), "col", 0, 0)
@@ -247,9 +254,9 @@
         target_potential.reshape(1, m),
     )
     stats = lax.all_to_all(stats, "col", 0, 0)
-    partial, f, h = call(
+    partial, h = call(
         functools.partial(backward_kernel, scale, target_count),
-        [(rows, width + rows, m // rows), (1, n), (1, n)],
+        [(rows, width + rows, m // rows), (1, n)],
         [keys, queries, means, pltpu.VMEM((rows, m // rows), F32)],
         2 * flops,
         x,
@@ -261,9 +268,9 @@
     pieces = [inverse] + [from_rows(inverse, rows, functools.partial(operator.xor, level), side) for level, side in ((0, 1), (1, 0), (1, 1))]
     four = jnp.concatenate(pieces, axis=0)
     pieces = [four] + [from_rows(four, rows, functools.partial(outward, hop), 0) for hop in HOPS]
-    plan, g = call(
-        functools.partial(plan_kernel, scale, source_count),
-        [(cols, width + 8, own), (1, m)],
+    (plan,) = call(
+        functools.partial(plan_kernel, scale),
+        [(cols, width + 8, own)],
         [keys, queries, means],
         2 * flops,
         x,
@@ -271,7 +278,18 @@
         h,
         lse,
     )
+    plan, h, lse = lax.optimization_barrier((plan, h, lse))
     plan = lax.all_to_all(plan, "col", 0, 0)
+    f, g = call(
+        functools.partial(potentials_kernel, scale, source_count),
+        [(1, n), (1, m)],
+        [],
+        1 << 20,
+        x,
+        target_points,
+        h,
+        lse,
+    )
     transport_map, inverse_map = call(finish_kernel, [(width, own), (width, m)], [], 1 << 20, plan, *pieces)
     return f.reshape(n), g.reshape(m), transport_map, inverse_map
 

time: 88.3 us -> 87.1 us (0.986)
    pallas_call x5 -> x6, Pallas kernels: 16.8 us -> 16.3 us  [call(): pl.pallas_call(body, out_shape=[jax.ShapeDtypeStruct(s, F32) for s in out...]
where the time goes in v5:
time: 87.1 us; the launch traced here: 86.8 us
  blocking collectives  50.1 us (58%)
  Pallas kernels  16.3 us (19%)
  starting transfers between devices  13.9 us (16%)
  waiting for transfers between devices  4.92 us (6%)
    all_to_all x1, blocking collectives, local(): partial = lax.all_to_all(partial, 'row', 0, 0)  21 us
    all_to_all x1, blocking collectives, local(): lax.all_to_all(jnp.broadcast_to(source_points, (cols, width, own)), 'col'...  17 us
    pallas_call x6, Pallas kernels, call(): pl.pallas_call(body, out_shape=[jax.ShapeDtypeStruct(s, F32) for s in out...  16.3 us
    all_to_all x1, blocking collectives, local(): stats = lax.all_to_all(stats, 'col', 0, 0)  12.1 us
    all_to_all x1, starting transfers between devices, local(): plan = lax.all_to_all(plan, 'col', 0, 0)  7.66 us
    ppermute x6, starting transfers between devices, from_rows(): lax.ppermute(value, 'row', [(level(r // 2) % levels * 2 + (r % 2 ^ side),...  6.27 us
    ppermute x6, waiting for transfers between devices, from_rows(): lax.ppermute(value, 'row', [(level(r // 2) % levels * 2 + (r % 2 ^ side),...  4.91 us
  transfers between devices with their start and end apart: 7, of which 2 were waited for; matrix products, arithmetic and copies ran while one was open for 0% of the time, Pallas kernels for 7%

profile of v5, /device:TPU:1, one launch (start us, length us, event | category | flops | bytes accessed | tf_op | source)
XLA Modules:
  0.0 86.8 jit_solution(7334691079926647737)
XLA Ops:
  0.6 0.7 broadcast_in_dim.3
  1.4 0.0 copy-start
  1.4 0.0 copy-start.1
  1.4 17.0 %all_to_all.20.x_ref = f32[16,32,128]{2,1,0:T(8,128)S(1)} all-to-all(f32[16,32,128]{2,1,0:T(8,128)S(1)} %broadcast_in_dim.3), channel_id=1, replica_groups=mesh['row'=16,'col'=16] {'col'}, dimensions={0} | all-to-all | bytes 524288 | tf_op jit(solution)/shard_map/all_to_all | solution.py:246
  18.4 0.0 copy-done
  18.4 0.0 copy-done.1
  18.4 3.6 %shard_map.66 = f32[16,2,2048]{2,1,0:T(2,128)S(1)} custom-call(f32[16,32,128]{2,1,0:T(8,128)S(1)} %all_to_all.20.x_ref, f32[32,2048]{1,0:T(8,128)S(1)} %copy-done, f32[1,2048]{1,0:T(1,128)S(1)} %bitcast.3), custom_call_target="tpu_custom_call" | custom-call | flops 2147483648 | bytes 1048576 | tf_op jit(solution)/shard_map/pallas_call | solution.py:223
  22.0 12.1 %all_to_all.21.stats_ref = f32[16,2,2048]{2,1,0:T(2,128)S(1)} all-to-all(f32[16,2,2048]{2,1,0:T(2,128)S(1)} %shard_map.66), channel_id=1, replica_groups=mesh['row'=16,'col'=16] {'col'}, dimensions={0} | all-to-all | bytes 524288 | tf_op jit(solution)/shard_map/all_to_all | solution.py:256
  34.2 5.7 %shard_map.67 = (f32[16,48,128]{2,1,0:T(8,128)S(1)}, f32[1,2048]{1,0:T(1,128)S(1)}) custom-call(f32[16,32,128]{2,1,0:T(8,128)S(1)} %all_to_all.20.x_ref, f32[32,2048]{1,0:T(8,128)S(1)} %copy-done, f32[16,2,2048]{2,1,0:T(2,128)S(1)} %all_to_all.21.stats_ref), custom_call_target="tpu_custom_call" | custom-call | flops 4294967296 | bytes 1048576 | tf_op jit(solution)/shard_map/pallas_call | solution.py:223
  39.8 21.0 %all_to_all.22.in_ref = f32[16,48,128]{2,1,0:T(8,128)S(1)} all-to-all(f32[16,48,128]{2,1,0:T(8,128)S(1)} %get-tuple-element.16), channel_id=1, replica_groups=mesh['row'=16,'col'=16] {'row'}, dimensions={0} | all-to-all | bytes 786432 | tf_op jit(solution)/shard_map/all_to_all | solution.py:266
  60.8 0.1 shard_map.68
  60.9 0.1 collective-permute-start.2
  61.0 1.3 %collective-permute-start.1 = (f32[32,128]{1,0:T(8,128)S(1)}, f32[32,128]{1,0:T(8,128)S(1)}, u32[]{:S(2)}, u32[]{:S(2)}) collective-permute-start(f32[32,128]{1,0:T(8,128)S(1)} %get-tuple-element.23), channel_id=1, source_target_pairs={{32,0},{48,16},{0,32},{16,48},{96,64},{112,80},{64,96},{80,112},{1... | collective-permute-start | bytes 49160 | tf_op jit(solution)/shard_map/ppermute | solution.py:194
  62.2 1.4 %collective-permute-start = (f32[32,128]{1,0:T(8,128)S(1)}, f32[32,128]{1,0:T(8,128)S(1)}, u32[]{:S(2)}, u32[]{:S(2)}) collective-permute-start(f32[32,128]{1,0:T(8,128)S(1)} %get-tuple-element.23), channel_id=1, source_target_pairs={{16,0},{0,16},{48,32},{32,48},{80,64},{64,80},{112,96},{96,112},{1... | collective-permute-start | bytes 49160 | tf_op jit(solution)/shard_map/ppermute | solution.py:194
  63.6 5.5 %shard_map.69 = f32[16,40,128]{2,1,0:T(8,128)} custom-call(f32[16,32,128]{2,1,0:T(8,128)S(1)} %all_to_all.20.x_ref, f32[32,2048]{1,0:T(8,128)S(1)} %copy-done, f32[1,2048]{1,0:T(1,128)S(1)} %get-tuple-element.18.h_ref, f32[16,128]{1,0:T(8,128)S(1)} %get-tuple-element.19.lse_ref), custom_call_target="tpu_custom_call" | custom-call | flops 4294967296 | bytes 1048576 | tf_op jit(solution)/shard_map/pallas_call | solution.py:223
  69.2 7.7 %all-to-all-start.3 = ((f32[16,40,128]{2,1,0:T(8,128)}), f32[16,40,128]{2,1,0:T(8,128)S(1)}, u32[]{:S(2)}, u32[]{:S(2)}) async-start(f32[16,40,128]{2,1,0:T(8,128)} %shard_map.69), calls=%async_computation.3 | async-start | bytes 655360 | tf_op jit(solution)/shard_map/all_to_all | solution.py:282
  76.8 0.0 collective-permute-done
  76.8 0.0 collective-permute-done.1
  76.9 0.0 collective-permute-done.2
  76.9 0.2 collective-permute-start.5
  77.1 3.1 %collective-permute-start.4 = (f32[128,128]{1,0:T(8,128)S(1)}, f32[128,128]{1,0:T(8,128)S(1)}, u32[]{:S(2)}, u32[]{:S(2)}) collective-permute-start(f32[128,128]{1,0:T(8,128)S(1)} %constant_dynamic-update-slice_fusion.refs_0_), channel_id=1, source_target_pairs={{64,0},{80,16},{224,32},{240,48},{128,64},{144,80},{32,96},{48,112... | collective-permute-start | bytes 196616 | tf_op jit(solution)/shard_map/ppermute | solution.py:194
  80.1 0.3 collective-permute-start.3
  80.4 0.7 shard_map.70
  81.1 3.0 %collective-permute-done.5.refs_3_ = f32[128,128]{1,0:T(8,128)S(1)} collective-permute-done((f32[128,128]{1,0:T(8,128)S(1)}, f32[128,128]{1,0:T(8,128)S(1)}, u32[]{:S(2)}, u32[]{:S(2)}) %collective-permute-start.5) | collective-permute-done | bytes 65568 | tf_op jit(solution)/shard_map/ppermute | solution.py:194
  84.1 0.0 collective-permute-done.4.refs_2_
  84.1 1.9 %collective-permute-done.3.refs_1_ = f32[128,128]{1,0:T(8,128)S(1)} collective-permute-done((f32[128,128]{1,0:T(8,128)S(1)}, f32[128,128]{1,0:T(8,128)S(1)}, u32[]{:S(2)}, u32[]{:S(2)}) %collective-permute-start.3) | collective-permute-done | bytes 65568 | tf_op jit(solution)/shard_map/ppermute | solution.py:194
  86.0 0.0 all-to-all-done.3.in_ref
  86.0 0.8 shard_map.71
  (4 shorter events, 0.0 us)
Async XLA Ops:
  1.4 17.1 %copy-start = (f32[32,2048]{1,0:T(8,128)S(1)}, f32[32,2048]{1,0:T(8,128)}, u32[]{:S(2)}) copy-start(f32[32,2048]{1,0:T(8,128)} %y_ref.7) | copy-start | bytes 786436
  1.4 17.1 %copy-start.1 = (f32[2048]{0:T(1024)S(1)}, f32[2048]{0:T(1024)}, u32[]{:S(2)}) copy-start(f32[2048]{0:T(1024)} %param.5) | copy-start | bytes 24580
  60.9 16.0 %collective-permute-start.2 = (f32[32,128]{1,0:T(8,128)S(1)}, f32[32,128]{1,0:T(8,128)S(1)}, u32[]{:S(2)}, u32[]{:S(2)}) collective-permute-start(f32[32,128]{1,0:T(8,128)S(1)} %get-tuple-element.23), channel_id=1, source_target_pairs={{48,0},{32,16},{16,32},{0,48},{112,64},{96,80},{80,96},{64,112},{1... | collective-permute-start | bytes 49160 | tf_op jit(solution)/shard_map/ppermute | solution.py:194
  61.0 15.9 %collective-permute-start.1 = (f32[32,128]{1,0:T(8,128)S(1)}, f32[32,128]{1,0:T(8,128)S(1)}, u32[]{:S(2)}, u32[]{:S(2)}) collective-permute-start(f32[32,128]{1,0:T(8,128)S(1)} %get-tuple-element.23), channel_id=1, source_target_pairs={{32,0},{48,16},{0,32},{16,48},{96,64},{112,80},{64,96},{80,112},{1... | collective-permute-start | bytes 49160 | tf_op jit(solution)/shard_map/ppermute | solution.py:194
  62.2 14.6 %collective-permute-start = (f32[32,128]{1,0:T(8,128)S(1)}, f32[32,128]{1,0:T(8,128)S(1)}, u32[]{:S(2)}, u32[]{:S(2)}) collective-permute-start(f32[32,128]{1,0:T(8,128)S(1)} %get-tuple-element.23), channel_id=1, source_target_pairs={{16,0},{0,16},{48,32},{32,48},{80,64},{64,80},{112,96},{96,112},{1... | collective-permute-start | bytes 49160 | tf_op jit(solution)/shard_map/ppermute | solution.py:194
  69.2 16.9 %all-to-all-start.3 = ((f32[16,40,128]{2,1,0:T(8,128)}), f32[16,40,128]{2,1,0:T(8,128)S(1)}, u32[]{:S(2)}, u32[]{:S(2)}) async-start(f32[16,40,128]{2,1,0:T(8,128)} %shard_map.69), calls=%async_computation.3 | async-start | bytes 655360 | tf_op jit(solution)/shard_map/all_to_all | solution.py:282
  76.9 7.3 %collective-permute-start.5 = (f32[128,128]{1,0:T(8,128)S(1)}, f32[128,128]{1,0:T(8,128)S(1)}, u32[]{:S(2)}, u32[]{:S(2)}) collective-permute-start(f32[128,128]{1,0:T(8,128)S(1)} %constant_dynamic-update-slice_fusion.refs_0_), channel_id=1, source_target_pairs={{160,0},{176,16},{128,32},{144,48},{224,64},{240,80},{192,96},{208... | collective-permute-start | bytes 196616 | tf_op jit(solution)/shard_map/ppermute | solution.py:194
  77.1 7.1 %collective-permute-start.4 = (f32[128,128]{1,0:T(8,128)S(1)}, f32[128,128]{1,0:T(8,128)S(1)}, u32[]{:S(2)}, u32[]{:S(2)}) collective-permute-start(f32[128,128]{1,0:T(8,128)S(1)} %constant_dynamic-update-slice_fusion.refs_0_), channel_id=1, source_target_pairs={{64,0},{80,16},{224,32},{240,48},{128,64},{144,80},{32,96},{48,112... | collective-permute-start | bytes 196616 | tf_op jit(solution)/shard_map/ppermute | solution.py:194
  80.1 5.9 %collective-permute-start.3 = (f32[128,128]{1,0:T(8,128)S(1)}, f32[128,128]{1,0:T(8,128)S(1)}, u32[]{:S(2)}, u32[]{:S(2)}) collective-permute-start(f32[128,128]{1,0:T(8,128)S(1)} %constant_dynamic-update-slice_fusion.refs_0_), channel_id=1, source_target_pairs={{224,0},{240,16},{64,32},{80,48},{32,64},{48,80},{128,96},{144,112... | collective-permute-start | bytes 196616 | tf_op jit(solution)/shard_map/ppermute | solution.py:194

commit v6 on v5

--- a/solution.py
+++ b/solution.py
@@ -16,7 +16,7 @@
 TILE = 256
 BLOCK = 512
 SMALL = 256
-HOPS = (1, -2, 3)
+HOPS = (-2, 1, 3)
 LOG2E = math.log2(math.e)
 VMEM_LIMIT = 48 * 1024 * 1024
 

time: 87.1 us -> 87.1 us (level)
  starting transfers between devices: 13.9 us -> 15.3 us
  waiting for transfers between devices: 4.92 us -> 3.59 us
    ppermute x6, waiting for transfers between devices: 4.91 us -> 1.95 us  [from_rows(): lax.ppermute(value, 'row', [(level(r // 2) % levels * 2 + (r % 2 ^ side),...]
    all_to_all x1, waiting for transfers between devices: 0.01 us -> 1.63 us  [local(): plan = lax.all_to_all(plan, 'col', 0, 0)]
    ppermute x6, starting transfers between devices: 6.27 us -> 7.6 us  [from_rows(): lax.ppermute(value, 'row', [(level(r // 2) % levels * 2 + (r % 2 ^ side),...]
  transfers between devices with their start and end apart: 7 -> 7, of which waited for: 2 -> 3; matrix products, arithmetic and copies ran while one was open for 0% -> 0% of each run, Pallas kernels for 7% -> 7%
where the time goes in v6:
time: 87.1 us; the launch traced here: 86.8 us
  blocking collectives  50.1 us (58%)
  Pallas kernels  16.3 us (19%)
  starting transfers between devices  15.3 us (18%)
  waiting for transfers between devices  3.59 us (4%)
    all_to_all x1, blocking collectives, local(): partial = lax.all_to_all(partial, 'row', 0, 0)  21 us
    all_to_all x1, blocking collectives, local(): lax.all_to_all(jnp.broadcast_to(source_points, (cols, width, own)), 'col'...  17 us
    pallas_call x6, Pallas kernels, call(): pl.pallas_call(body, out_shape=[jax.ShapeDtypeStruct(s, F32) for s in out...  16.3 us
    all_to_all x1, blocking collectives, local(): stats = lax.all_to_all(stats, 'col', 0, 0)  12.1 us
    all_to_all x1, starting transfers between devices, local(): plan = lax.all_to_all(plan, 'col', 0, 0)  7.66 us
    ppermute x6, starting transfers between devices, from_rows(): lax.ppermute(value, 'row', [(level(r // 2) % levels * 2 + (r % 2 ^ side),...  7.6 us
    ppermute x6, waiting for transfers between devices, from_rows(): lax.ppermute(value, 'row', [(level(r // 2) % levels * 2 + (r % 2 ^ side),...  1.95 us
  transfers between devices with their start and end apart: 7, of which 3 were waited for; matrix products, arithmetic and copies ran while one was open for 0% of the time, Pallas kernels for 7%

profile of v6, /device:TPU:1, one launch (start us, length us, event | category | flops | bytes accessed | tf_op | source)
XLA Modules:
  0.0 86.8 jit_solution(7349903524990001999)
XLA Ops:
  0.6 0.7 broadcast_in_dim.3
  1.4 0.0 copy-start
  1.4 0.0 copy-start.1
  1.4 17.0 %all_to_all.20.x_ref = f32[16,32,128]{2,1,0:T(8,128)S(1)} all-to-all(f32[16,32,128]{2,1,0:T(8,128)S(1)} %broadcast_in_dim.3), channel_id=1, replica_groups=mesh['row'=16,'col'=16] {'col'}, dimensions={0} | all-to-all | bytes 524288 | tf_op jit(solution)/shard_map/all_to_all | solution.py:246
  18.4 0.0 copy-done
  18.4 0.0 copy-done.1
  18.4 3.6 %shard_map.66 = f32[16,2,2048]{2,1,0:T(2,128)S(1)} custom-call(f32[16,32,128]{2,1,0:T(8,128)S(1)} %all_to_all.20.x_ref, f32[32,2048]{1,0:T(8,128)S(1)} %copy-done, f32[1,2048]{1,0:T(1,128)S(1)} %bitcast.3), custom_call_target="tpu_custom_call" | custom-call | flops 2147483648 | bytes 1048576 | tf_op jit(solution)/shard_map/pallas_call | solution.py:223
  22.0 12.1 %all_to_all.21.stats_ref = f32[16,2,2048]{2,1,0:T(2,128)S(1)} all-to-all(f32[16,2,2048]{2,1,0:T(2,128)S(1)} %shard_map.66), channel_id=1, replica_groups=mesh['row'=16,'col'=16] {'col'}, dimensions={0} | all-to-all | bytes 524288 | tf_op jit(solution)/shard_map/all_to_all | solution.py:256
  34.2 5.7 %shard_map.67 = (f32[16,48,128]{2,1,0:T(8,128)S(1)}, f32[1,2048]{1,0:T(1,128)S(1)}) custom-call(f32[16,32,128]{2,1,0:T(8,128)S(1)} %all_to_all.20.x_ref, f32[32,2048]{1,0:T(8,128)S(1)} %copy-done, f32[16,2,2048]{2,1,0:T(2,128)S(1)} %all_to_all.21.stats_ref), custom_call_target="tpu_custom_call" | custom-call | flops 4294967296 | bytes 1048576 | tf_op jit(solution)/shard_map/pallas_call | solution.py:223
  39.8 21.0 %all_to_all.22.in_ref = f32[16,48,128]{2,1,0:T(8,128)S(1)} all-to-all(f32[16,48,128]{2,1,0:T(8,128)S(1)} %get-tuple-element.16), channel_id=1, replica_groups=mesh['row'=16,'col'=16] {'row'}, dimensions={0} | all-to-all | bytes 786432 | tf_op jit(solution)/shard_map/all_to_all | solution.py:266
  60.8 0.1 shard_map.68
  60.9 0.1 collective-permute-start.2
  61.0 1.3 %collective-permute-start.1 = (f32[32,128]{1,0:T(8,128)S(1)}, f32[32,128]{1,0:T(8,128)S(1)}, u32[]{:S(2)}, u32[]{:S(2)}) collective-permute-start(f32[32,128]{1,0:T(8,128)S(1)} %get-tuple-element.23), channel_id=1, source_target_pairs={{32,0},{48,16},{0,32},{16,48},{96,64},{112,80},{64,96},{80,112},{1... | collective-permute-start | bytes 49160 | tf_op jit(solution)/shard_map/ppermute | solution.py:194
  62.2 1.4 %collective-permute-start = (f32[32,128]{1,0:T(8,128)S(1)}, f32[32,128]{1,0:T(8,128)S(1)}, u32[]{:S(2)}, u32[]{:S(2)}) collective-permute-start(f32[32,128]{1,0:T(8,128)S(1)} %get-tuple-element.23), channel_id=1, source_target_pairs={{16,0},{0,16},{48,32},{32,48},{80,64},{64,80},{112,96},{96,112},{1... | collective-permute-start | bytes 49160 | tf_op jit(solution)/shard_map/ppermute | solution.py:194
  63.6 5.5 %shard_map.69 = f32[16,40,128]{2,1,0:T(8,128)} custom-call(f32[16,32,128]{2,1,0:T(8,128)S(1)} %all_to_all.20.x_ref, f32[32,2048]{1,0:T(8,128)S(1)} %copy-done, f32[1,2048]{1,0:T(1,128)S(1)} %get-tuple-element.18.h_ref, f32[16,128]{1,0:T(8,128)S(1)} %get-tuple-element.19.lse_ref), custom_call_target="tpu_custom_call" | custom-call | flops 4294967296 | bytes 1048576 | tf_op jit(solution)/shard_map/pallas_call | solution.py:223
  69.2 7.7 %all-to-all-start.3 = ((f32[16,40,128]{2,1,0:T(8,128)}), f32[16,40,128]{2,1,0:T(8,128)S(1)}, u32[]{:S(2)}, u32[]{:S(2)}) async-start(f32[16,40,128]{2,1,0:T(8,128)} %shard_map.69), calls=%async_computation.3 | async-start | bytes 655360 | tf_op jit(solution)/shard_map/all_to_all | solution.py:282
  76.8 0.0 collective-permute-done
  76.8 0.0 collective-permute-done.1
  76.9 0.0 collective-permute-done.2
  76.9 0.2 collective-permute-start.5
  77.1 2.6 %collective-permute-start.4 = (f32[128,128]{1,0:T(8,128)S(1)}, f32[128,128]{1,0:T(8,128)S(1)}, u32[]{:S(2)}, u32[]{:S(2)}) collective-permute-start(f32[128,128]{1,0:T(8,128)S(1)} %constant_dynamic-update-slice_fusion.refs_0_), channel_id=1, source_target_pairs={{224,0},{240,16},{64,32},{80,48},{32,64},{48,80},{128,96},{144,112... | collective-permute-start | bytes 196616 | tf_op jit(solution)/shard_map/ppermute | solution.py:194
  79.6 2.1 %collective-permute-start.3 = (f32[128,128]{1,0:T(8,128)S(1)}, f32[128,128]{1,0:T(8,128)S(1)}, u32[]{:S(2)}, u32[]{:S(2)}) collective-permute-start(f32[128,128]{1,0:T(8,128)S(1)} %constant_dynamic-update-slice_fusion.refs_0_), channel_id=1, source_target_pairs={{64,0},{80,16},{224,32},{240,48},{128,64},{144,80},{32,96},{48,112... | collective-permute-start | bytes 196616 | tf_op jit(solution)/shard_map/ppermute | solution.py:194
  81.8 0.7 shard_map.70
  82.4 1.7 %collective-permute-done.5.refs_3_ = f32[128,128]{1,0:T(8,128)S(1)} collective-permute-done((f32[128,128]{1,0:T(8,128)S(1)}, f32[128,128]{1,0:T(8,128)S(1)}, u32[]{:S(2)}, u32[]{:S(2)}) %collective-permute-start.5) | collective-permute-done | bytes 65568 | tf_op jit(solution)/shard_map/ppermute | solution.py:194
  84.1 0.2 collective-permute-done.4.refs_2_
  84.4 0.0 collective-permute-done.3.refs_1_
  84.4 1.6 %all-to-all-done.3.in_ref = f32[16,40,128]{2,1,0:T(8,128)S(1)} async-done(((f32[16,40,128]{2,1,0:T(8,128)}), f32[16,40,128]{2,1,0:T(8,128)S(1)}, u32[]{:S(2)}, u32[]{:S(2)}) %all-to-all-start.3) | async-done | bytes 327712 | tf_op jit(solution)/shard_map/all_to_all | solution.py:282
  86.0 0.8 shard_map.71
  (4 shorter events, 0.0 us)
Async XLA Ops:
  1.4 17.1 %copy-start = (f32[32,2048]{1,0:T(8,128)S(1)}, f32[32,2048]{1,0:T(8,128)}, u32[]{:S(2)}) copy-start(f32[32,2048]{1,0:T(8,128)} %y_ref.7) | copy-start | bytes 786436
  1.4 17.1 %copy-start.1 = (f32[2048]{0:T(1024)S(1)}, f32[2048]{0:T(1024)}, u32[]{:S(2)}) copy-start(f32[2048]{0:T(1024)} %param.5) | copy-start | bytes 24580
  60.9 16.0 %collective-permute-start.2 = (f32[32,128]{1,0:T(8,128)S(1)}, f32[32,128]{1,0:T(8,128)S(1)}, u32[]{:S(2)}, u32[]{:S(2)}) collective-permute-start(f32[32,128]{1,0:T(8,128)S(1)} %get-tuple-element.23), channel_id=1, source_target_pairs={{48,0},{32,16},{16,32},{0,48},{112,64},{96,80},{80,96},{64,112},{1... | collective-permute-start | bytes 49160 | tf_op jit(solution)/shard_map/ppermute | solution.py:194
  61.0 15.9 %collective-permute-start.1 = (f32[32,128]{1,0:T(8,128)S(1)}, f32[32,128]{1,0:T(8,128)S(1)}, u32[]{:S(2)}, u32[]{:S(2)}) collective-permute-start(f32[32,128]{1,0:T(8,128)S(1)} %get-tuple-element.23), channel_id=1, source_target_pairs={{32,0},{48,16},{0,32},{16,48},{96,64},{112,80},{64,96},{80,112},{1... | collective-permute-start | bytes 49160 | tf_op jit(solution)/shard_map/ppermute | solution.py:194
  62.2 14.6 %collective-permute-start = (f32[32,128]{1,0:T(8,128)S(1)}, f32[32,128]{1,0:T(8,128)S(1)}, u32[]{:S(2)}, u32[]{:S(2)}) collective-permute-start(f32[32,128]{1,0:T(8,128)S(1)} %get-tuple-element.23), channel_id=1, source_target_pairs={{16,0},{0,16},{48,32},{32,48},{80,64},{64,80},{112,96},{96,112},{1... | collective-permute-start | bytes 49160 | tf_op jit(solution)/shard_map/ppermute | solution.py:194
  69.2 16.9 %all-to-all-start.3 = ((f32[16,40,128]{2,1,0:T(8,128)}), f32[16,40,128]{2,1,0:T(8,128)S(1)}, u32[]{:S(2)}, u32[]{:S(2)}) async-start(f32[16,40,128]{2,1,0:T(8,128)} %shard_map.69), calls=%async_computation.3 | async-start | bytes 655360 | tf_op jit(solution)/shard_map/all_to_all | solution.py:282
  76.9 7.3 %collective-permute-start.5 = (f32[128,128]{1,0:T(8,128)S(1)}, f32[128,128]{1,0:T(8,128)S(1)}, u32[]{:S(2)}, u32[]{:S(2)}) collective-permute-start(f32[128,128]{1,0:T(8,128)S(1)} %constant_dynamic-update-slice_fusion.refs_0_), channel_id=1, source_target_pairs={{160,0},{176,16},{128,32},{144,48},{224,64},{240,80},{192,96},{208... | collective-permute-start | bytes 196616 | tf_op jit(solution)/shard_map/ppermute | solution.py:194
  77.1 7.3 %collective-permute-start.4 = (f32[128,128]{1,0:T(8,128)S(1)}, f32[128,128]{1,0:T(8,128)S(1)}, u32[]{:S(2)}, u32[]{:S(2)}) collective-permute-start(f32[128,128]{1,0:T(8,128)S(1)} %constant_dynamic-update-slice_fusion.refs_0_), channel_id=1, source_target_pairs={{224,0},{240,16},{64,32},{80,48},{32,64},{48,80},{128,96},{144,112... | collective-permute-start | bytes 196616 | tf_op jit(solution)/shard_map/ppermute | solution.py:194
  79.6 4.8 %collective-permute-start.3 = (f32[128,128]{1,0:T(8,128)S(1)}, f32[128,128]{1,0:T(8,128)S(1)}, u32[]{:S(2)}, u32[]{:S(2)}) collective-permute-start(f32[128,128]{1,0:T(8,128)S(1)} %constant_dynamic-update-slice_fusion.refs_0_), channel_id=1, source_target_pairs={{64,0},{80,16},{224,32},{240,48},{128,64},{144,80},{32,96},{48,112... | collective-permute-start | bytes 196616 | tf_op jit(solution)/shard_map/ppermute | solution.py:194

commit v7 on v6

--- a/solution.py
+++ b/solution.py
@@ -15,7 +15,7 @@
 LANES = 128
 TILE = 256
 BLOCK = 512
-SMALL = 256
+SMALL = 128
 HOPS = (-2, 1, 3)
 LOG2E = math.log2(math.e)
 VMEM_LIMIT = 48 * 1024 * 1024

time: 87.1 us -> 87 us (level)
  no operation moved by 1% of the time
where the time goes in v7:
time: 87 us; the launch traced here: 86.6 us
  blocking collectives  50.1 us (58%)
  Pallas kernels  16.2 us (19%)
  starting transfers between devices  15.3 us (18%)
  waiting for transfers between devices  3.59 us (4%)
    all_to_all x1, blocking collectives, local(): partial = lax.all_to_all(partial, 'row', 0, 0)  21 us
    all_to_all x1, blocking collectives, local(): lax.all_to_all(jnp.broadcast_to(source_points, (cols, width, own)), 'col'...  17 us
    pallas_call x6, Pallas kernels, call(): pl.pallas_call(body, out_shape=[jax.ShapeDtypeStruct(s, F32) for s in out...  16.2 us
    all_to_all x1, blocking collectives, local(): stats = lax.all_to_all(stats, 'col', 0, 0)  12.1 us
    all_to_all x1, starting transfers between devices, local(): plan = lax.all_to_all(plan, 'col', 0, 0)  7.66 us
    ppermute x6, starting transfers between devices, from_rows(): lax.ppermute(value, 'row', [(level(r // 2) % levels * 2 + (r % 2 ^ side),...  7.6 us
    ppermute x6, waiting for transfers between devices, from_rows(): lax.ppermute(value, 'row', [(level(r // 2) % levels * 2 + (r % 2 ^ side),...  1.95 us
  transfers between devices with their start and end apart: 7, of which 3 were waited for; matrix products, arithmetic and copies ran while one was open for 0% of the time, Pallas kernels for 7%

profile of v7, /device:TPU:1, one launch (start us, length us, event | category | flops | bytes accessed | tf_op | source)
XLA Modules:
  0.0 86.6 jit_solution(863395585386907512)
XLA Ops:
  0.6 0.7 broadcast_in_dim.3
  1.4 0.0 copy-start
  1.4 0.0 copy-start.1
  1.4 17.0 %all_to_all.20.x_ref = f32[16,32,128]{2,1,0:T(8,128)S(1)} all-to-all(f32[16,32,128]{2,1,0:T(8,128)S(1)} %broadcast_in_dim.3), channel_id=1, replica_groups=mesh['row'=16,'col'=16] {'col'}, dimensions={0} | all-to-all | bytes 524288 | tf_op jit(solution)/shard_map/all_to_all | solution.py:246
  18.4 0.0 copy-done
  18.4 0.0 copy-done.1
  18.4 3.4 %shard_map.66 = f32[16,2,2048]{2,1,0:T(2,128)S(1)} custom-call(f32[16,32,128]{2,1,0:T(8,128)S(1)} %all_to_all.20.x_ref, f32[32,2048]{1,0:T(8,128)S(1)} %copy-done, f32[1,2048]{1,0:T(1,128)S(1)} %bitcast.3), custom_call_target="tpu_custom_call" | custom-call | flops 2147483648 | bytes 1048576 | tf_op jit(solution)/shard_map/pallas_call | solution.py:223
  21.9 12.1 %all_to_all.21.stats_ref = f32[16,2,2048]{2,1,0:T(2,128)S(1)} all-to-all(f32[16,2,2048]{2,1,0:T(2,128)S(1)} %shard_map.66), channel_id=1, replica_groups=mesh['row'=16,'col'=16] {'col'}, dimensions={0} | all-to-all | bytes 524288 | tf_op jit(solution)/shard_map/all_to_all | solution.py:256
  34.0 5.7 %shard_map.67 = (f32[16,48,128]{2,1,0:T(8,128)S(1)}, f32[1,2048]{1,0:T(1,128)S(1)}) custom-call(f32[16,32,128]{2,1,0:T(8,128)S(1)} %all_to_all.20.x_ref, f32[32,2048]{1,0:T(8,128)S(1)} %copy-done, f32[16,2,2048]{2,1,0:T(2,128)S(1)} %all_to_all.21.stats_ref), custom_call_target="tpu_custom_call" | custom-call | flops 4294967296 | bytes 1048576 | tf_op jit(solution)/shard_map/pallas_call | solution.py:223
  39.7 21.0 %all_to_all.22.in_ref = f32[16,48,128]{2,1,0:T(8,128)S(1)} all-to-all(f32[16,48,128]{2,1,0:T(8,128)S(1)} %get-tuple-element.16), channel_id=1, replica_groups=mesh['row'=16,'col'=16] {'row'}, dimensions={0} | all-to-all | bytes 786432 | tf_op jit(solution)/shard_map/all_to_all | solution.py:266
  60.6 0.1 shard_map.68
  60.7 0.1 collective-permute-start.2
  60.8 1.3 %collective-permute-start.1 = (f32[32,128]{1,0:T(8,128)S(1)}, f32[32,128]{1,0:T(8,128)S(1)}, u32[]{:S(2)}, u32[]{:S(2)}) collective-permute-start(f32[32,128]{1,0:T(8,128)S(1)} %get-tuple-element.23), channel_id=1, source_target_pairs={{32,0},{48,16},{0,32},{16,48},{96,64},{112,80},{64,96},{80,112},{1... | collective-permute-start | bytes 49160 | tf_op jit(solution)/shard_map/ppermute | solution.py:194
  62.1 1.4 %collective-permute-start = (f32[32,128]{1,0:T(8,128)S(1)}, f32[32,128]{1,0:T(8,128)S(1)}, u32[]{:S(2)}, u32[]{:S(2)}) collective-permute-start(f32[32,128]{1,0:T(8,128)S(1)} %get-tuple-element.23), channel_id=1, source_target_pairs={{16,0},{0,16},{48,32},{32,48},{80,64},{64,80},{112,96},{96,112},{1... | collective-permute-start | bytes 49160 | tf_op jit(solution)/shard_map/ppermute | solution.py:194
  63.5 5.5 %shard_map.69 = f32[16,40,128]{2,1,0:T(8,128)} custom-call(f32[16,32,128]{2,1,0:T(8,128)S(1)} %all_to_all.20.x_ref, f32[32,2048]{1,0:T(8,128)S(1)} %copy-done, f32[1,2048]{1,0:T(1,128)S(1)} %get-tuple-element.18.h_ref, f32[16,128]{1,0:T(8,128)S(1)} %get-tuple-element.19.lse_ref), custom_call_target="tpu_custom_call" | custom-call | flops 4294967296 | bytes 1048576 | tf_op jit(solution)/shard_map/pallas_call | solution.py:223
  69.0 7.7 %all-to-all-start.3 = ((f32[16,40,128]{2,1,0:T(8,128)}), f32[16,40,128]{2,1,0:T(8,128)S(1)}, u32[]{:S(2)}, u32[]{:S(2)}) async-start(f32[16,40,128]{2,1,0:T(8,128)} %shard_map.69), calls=%async_computation.3 | async-start | bytes 655360 | tf_op jit(solution)/shard_map/all_to_all | solution.py:282
  76.7 0.0 collective-permute-done
  76.7 0.0 collective-permute-done.1
  76.7 0.0 collective-permute-done.2
  76.7 0.2 collective-permute-start.5
  76.9 2.6 %collective-permute-start.4 = (f32[128,128]{1,0:T(8,128)S(1)}, f32[128,128]{1,0:T(8,128)S(1)}, u32[]{:S(2)}, u32[]{:S(2)}) collective-permute-start(f32[128,128]{1,0:T(8,128)S(1)} %constant_dynamic-update-slice_fusion.refs_0_), channel_id=1, source_target_pairs={{224,0},{240,16},{64,32},{80,48},{32,64},{48,80},{128,96},{144,112... | collective-permute-start | bytes 196616 | tf_op jit(solution)/shard_map/ppermute | solution.py:194
  79.5 2.1 %collective-permute-start.3 = (f32[128,128]{1,0:T(8,128)S(1)}, f32[128,128]{1,0:T(8,128)S(1)}, u32[]{:S(2)}, u32[]{:S(2)}) collective-permute-start(f32[128,128]{1,0:T(8,128)S(1)} %constant_dynamic-update-slice_fusion.refs_0_), channel_id=1, source_target_pairs={{64,0},{80,16},{224,32},{240,48},{128,64},{144,80},{32,96},{48,112... | collective-permute-start | bytes 196616 | tf_op jit(solution)/shard_map/ppermute | solution.py:194
  81.6 0.7 shard_map.70
  82.3 1.7 %collective-permute-done.5.refs_3_ = f32[128,128]{1,0:T(8,128)S(1)} collective-permute-done((f32[128,128]{1,0:T(8,128)S(1)}, f32[128,128]{1,0:T(8,128)S(1)}, u32[]{:S(2)}, u32[]{:S(2)}) %collective-permute-start.5) | collective-permute-done | bytes 65568 | tf_op jit(solution)/shard_map/ppermute | solution.py:194
  84.0 0.2 collective-permute-done.4.refs_2_
  84.2 0.0 collective-permute-done.3.refs_1_
  84.2 1.6 %all-to-all-done.3.in_ref = f32[16,40,128]{2,1,0:T(8,128)S(1)} async-done(((f32[16,40,128]{2,1,0:T(8,128)}), f32[16,40,128]{2,1,0:T(8,128)S(1)}, u32[]{:S(2)}, u32[]{:S(2)}) %all-to-all-start.3) | async-done | bytes 327712 | tf_op jit(solution)/shard_map/all_to_all | solution.py:282
  85.9 0.8 shard_map.71
  (4 shorter events, 0.0 us)
Async XLA Ops:
  1.4 17.1 %copy-start = (f32[32,2048]{1,0:T(8,128)S(1)}, f32[32,2048]{1,0:T(8,128)}, u32[]{:S(2)}) copy-start(f32[32,2048]{1,0:T(8,128)} %y_ref.7) | copy-start | bytes 786436
  1.4 17.1 %copy-start.1 = (f32[2048]{0:T(1024)S(1)}, f32[2048]{0:T(1024)}, u32[]{:S(2)}) copy-start(f32[2048]{0:T(1024)} %param.5) | copy-start | bytes 24580
  60.7 16.0 %collective-permute-start.2 = (f32[32,128]{1,0:T(8,128)S(1)}, f32[32,128]{1,0:T(8,128)S(1)}, u32[]{:S(2)}, u32[]{:S(2)}) collective-permute-start(f32[32,128]{1,0:T(8,128)S(1)} %get-tuple-element.23), channel_id=1, source_target_pairs={{48,0},{32,16},{16,32},{0,48},{112,64},{96,80},{80,96},{64,112},{1... | collective-permute-start | bytes 49160 | tf_op jit(solution)/shard_map/ppermute | solution.py:194
  60.8 15.9 %collective-permute-start.1 = (f32[32,128]{1,0:T(8,128)S(1)}, f32[32,128]{1,0:T(8,128)S(1)}, u32[]{:S(2)}, u32[]{:S(2)}) collective-permute-start(f32[32,128]{1,0:T(8,128)S(1)} %get-tuple-element.23), channel_id=1, source_target_pairs={{32,0},{48,16},{0,32},{16,48},{96,64},{112,80},{64,96},{80,112},{1... | collective-permute-start | bytes 49160 | tf_op jit(solution)/shard_map/ppermute | solution.py:194
  62.1 14.6 %collective-permute-start = (f32[32,128]{1,0:T(8,128)S(1)}, f32[32,128]{1,0:T(8,128)S(1)}, u32[]{:S(2)}, u32[]{:S(2)}) collective-permute-start(f32[32,128]{1,0:T(8,128)S(1)} %get-tuple-element.23), channel_id=1, source_target_pairs={{16,0},{0,16},{48,32},{32,48},{80,64},{64,80},{112,96},{96,112},{1... | collective-permute-start | bytes 49160 | tf_op jit(solution)/shard_map/ppermute | solution.py:194
  69.0 16.9 %all-to-all-start.3 = ((f32[16,40,128]{2,1,0:T(8,128)}), f32[16,40,128]{2,1,0:T(8,128)S(1)}, u32[]{:S(2)}, u32[]{:S(2)}) async-start(f32[16,40,128]{2,1,0:T(8,128)} %shard_map.69), calls=%async_computation.3 | async-start | bytes 655360 | tf_op jit(solution)/shard_map/all_to_all | solution.py:282
  76.7 7.3 %collective-permute-start.5 = (f32[128,128]{1,0:T(8,128)S(1)}, f32[128,128]{1,0:T(8,128)S(1)}, u32[]{:S(2)}, u32[]{:S(2)}) collective-permute-start(f32[128,128]{1,0:T(8,128)S(1)} %constant_dynamic-update-slice_fusion.refs_0_), channel_id=1, source_target_pairs={{160,0},{176,16},{128,32},{144,48},{224,64},{240,80},{192,96},{208... | collective-permute-start | bytes 196616 | tf_op jit(solution)/shard_map/ppermute | solution.py:194
  76.9 7.3 %collective-permute-start.4 = (f32[128,128]{1,0:T(8,128)S(1)}, f32[128,128]{1,0:T(8,128)S(1)}, u32[]{:S(2)}, u32[]{:S(2)}) collective-permute-start(f32[128,128]{1,0:T(8,128)S(1)} %constant_dynamic-update-slice_fusion.refs_0_), channel_id=1, source_target_pairs={{224,0},{240,16},{64,32},{80,48},{32,64},{48,80},{128,96},{144,112... | collective-permute-start | bytes 196616 | tf_op jit(solution)/shard_map/ppermute | solution.py:194
  79.5 4.8 %collective-permute-start.3 = (f32[128,128]{1,0:T(8,128)S(1)}, f32[128,128]{1,0:T(8,128)S(1)}, u32[]{:S(2)}, u32[]{:S(2)}) collective-permute-start(f32[128,128]{1,0:T(8,128)S(1)} %constant_dynamic-update-slice_fusion.refs_0_), channel_id=1, source_target_pairs={{64,0},{80,16},{224,32},{240,48},{128,64},{144,80},{32,96},{48,112... | collective-permute-start | bytes 196616 | tf_op jit(solution)/shard_map/ppermute | solution.py:194
